TPU v7x, 32 devices: a whole 2x2x4 slice. The times are simulated.
32 devices in a mesh: groups: 2 (over y), owner: 16 (over z, x, core).
Axes of the slice: x: 2, y: 2, z: 4, core: 2. Of those that a mesh axis runs over, the one named last changes fastest.
Arguments:
- tokens: bfloat16 [4096, 8192], P(('groups', 'owner')), parts along dimension 0, may hold values from -0.59765625 to 0.59765625
- task_ids: int32 [4096, 1], P(('groups', 'owner')), parts along dimension 0, may hold values from 0 to 15, as said below
- cotangent: bfloat16 [4096, 8192], P(('groups', 'owner')), parts along dimension 0, may hold values from -0.75 to 0.75
- down_factors: bfloat16 [16, 64, 8192], P('owner'), may hold values from -0.75 to 0.75
- up_factors: bfloat16 [16, 64, 8192], P('owner'), may hold values from -0.75 to 0.75
Outputs:
- adapter_out: bfloat16 [4096, 8192], P(('groups', 'owner')), parts along dimension 0
- input_grad: bfloat16 [4096, 8192], P(('groups', 'owner')), parts along dimension 0
- down_grad: bfloat16 [32, 64, 8192], P(('groups', 'owner')), parts along dimension 0
- up_grad: bfloat16 [32, 64, 8192], P(('groups', 'owner')), parts along dimension 0
There are 2 independent parts, one for each index of `groups`. A program takes and returns all parts, laid end to end along the dimension named above; an argument that names none is the same for every part. Nothing has to cross between parts.
Inputs may be any that keep to these rules, and one draw needn't show every extreme that they name: `task_ids`: on every device, one adapter (the same on all devices) has exactly 24 of the device's 128 tokens; every other adapter has at most 8 tokens on a device, and on every device some other adapter has exactly 8.
All inputs are finite; a program needn't handle non-finite values.
Results may differ from a plain program's by a relative error of at most 0.005.
Values may be sent and summed in bfloat16 or wider, within the bound.
A program may use at most 128 MiB of HBM per device.

v0:
```python
import jax
import jax.numpy as jnp
from jax import lax
from jax.sharding import PartitionSpec as P


def branch(rows_in, rows_cot, down_mat, up_mat):
    hidden = lax.dot_general(
        rows_in, down_mat, (((1,), (1,)), ((), ())), preferred_element_type=jnp.float32
    )
    sig_hidden = jax.nn.sigmoid(hidden)
    activated = (hidden * sig_hidden).astype(jnp.bfloat16)
    result = jnp.dot(activated, up_mat, preferred_element_type=jnp.float32).astype(jnp.bfloat16)
    act_grad = lax.dot_general(
        rows_cot, up_mat, (((1,), (1,)), ((), ())), preferred_element_type=jnp.float32
    )
    hid_grad = (act_grad * sig_hidden * (1.0 + hidden * (1.0 - sig_hidden))).astype(jnp.bfloat16)
    in_grad = jnp.dot(hid_grad, down_mat, preferred_element_type=jnp.float32).astype(jnp.bfloat16)
    down_sum = lax.dot_general(
        hid_grad, rows_in, (((0,), (0,)), ((), ())), preferred_element_type=jnp.float32
    )
    up_sum = lax.dot_general(
        activated, rows_cot, (((0,), (0,)), ((), ())), preferred_element_type=jnp.float32
    )
    return (result, in_grad, down_sum, up_sum)


def on_device(tokens, task_ids, cotangent, down_factors, up_factors):
    owners = lax.axis_size("owner")
    tok_count, model_width = tokens.shape
    cold_cap = tok_count // owners
    busy_cap = 3 * cold_cap
    task_of = task_ids[:, 0]
    onehot = (task_of[:, None] == jnp.arange(owners, dtype=jnp.int32)[None, :]).astype(jnp.int32)
    running = jnp.cumsum(onehot, axis=0)
    rank_in = jnp.sum(onehot * (running - 1), axis=1)
    down_mat = down_factors[0]
    up_mat = up_factors[0]
    slot_of = task_of * busy_cap + rank_in
    send_rows = jnp.zeros((owners * busy_cap, model_width), tokens.dtype).at[slot_of].set(tokens)
    send_cot = (
        jnp.zeros((owners * busy_cap, model_width), cotangent.dtype).at[slot_of].set(cotangent)
    )
    got_rows, got_cot = (
        lax.all_to_all(
            send_rows.reshape(owners, busy_cap, model_width),
            "owner",
            split_axis=0,
            concat_axis=0,
            tiled=True,
        ),
        lax.all_to_all(
            send_cot.reshape(owners, busy_cap, model_width),
            "owner",
            split_axis=0,
            concat_axis=0,
            tiled=True,
        ),
    )
    result, in_grad, down_sum, up_sum = branch(
        got_rows.reshape(-1, model_width), got_cot.reshape(-1, model_width), down_mat, up_mat
    )
    back_out, back_grad = (
        lax.all_to_all(
            result.reshape(owners, busy_cap, model_width),
            "owner",
            split_axis=0,
            concat_axis=0,
            tiled=True,
        ),
        lax.all_to_all(
            in_grad.reshape(owners, busy_cap, model_width),
            "owner",
            split_axis=0,
            concat_axis=0,
            tiled=True,
        ),
    )
    adapter_out = back_out.reshape(-1, model_width)[slot_of]
    input_grad = back_grad.reshape(-1, model_width)[slot_of]
    return (
        adapter_out,
        input_grad,
        down_sum.astype(jnp.bfloat16)[None],
        up_sum.astype(jnp.bfloat16)[None],
    )


def solution(mesh):
    placed = (
        P(("groups", "owner"), None),
        P(("groups", "owner"), None),
        P(("groups", "owner"), None),
        P("owner", None, None),
        P("owner", None, None),
    )
    return jax.shard_map(
        on_device,
        mesh=mesh,
        in_specs=placed,
        out_specs=(
            P(("groups", "owner"), None),
            P(("groups", "owner"), None),
            P(("groups", "owner"), None, None),
            P(("groups", "owner"), None, None),
        ),
        check_vma=False,
    )
```

profile of v0, /device:TPU:11, one launch (start us, length us, event | category | flops | bytes accessed | tf_op | source)
XLA Modules:
  0.0 591.1 jit_solution(15259812658324419971)
XLA Ops:
  0.6 0.0 copy-start
  0.6 0.8 fusion.13
  1.5 0.2 reduce_window_sum.11
  1.6 0.8 select_reduce_fusion
  2.5 0.7 fusion.14
  3.1 8.2 %scatter_custom_fusion = bf16[384,8192]{1,0:T(8,128)(2,1)} fusion(s32[128]{0:T(128)S(1)} %fusion.14, bf16[128,8192]{1,0:T(8,128)(2,1)} %param.5, bf16[]{:T(256)} %constant.6.clone.1), kind=kCustom, calls=%fused_computation.12 | custom fusion | bytes 6291968 | tf_op jit(solution)/shard_map/scatter | solution.py:40
  11.3 6.6 %all-to-all-start = ((bf16[16,24,8192]{2,1,0:T(8,128)(2,1)}), bf16[16,24,8192]{2,1,0:T(8,128)(2,1)}, u32[]{:S(2)}, u32[]{:S(2)}) async-start(bf16[16,24,8192]{2,1,0:T(8,128)(2,1)} %bitcast.40), calls=%async_computation | async-start | bytes 12582912 | tf_op jit(solution)/shard_map/all_to_all | solution.py:45
  17.9 8.1 %scatter_custom_fusion.1 = bf16[384,8192]{1,0:T(8,128)(2,1)} fusion(s32[128]{0:T(128)S(1)} %fusion.14, bf16[128,8192]{1,0:T(8,128)(2,1)} %param.7, bf16[]{:T(256)} %constant.6.clone.1), kind=kCustom, calls=%fused_computation.10 | custom fusion | bytes 6291968 | tf_op jit(solution)/shard_map/scatter | solution.py:42
  26.0 129.3 %all-to-all-done = bf16[16,24,8192]{2,1,0:T(8,128)(2,1)} async-done(((bf16[16,24,8192]{2,1,0:T(8,128)(2,1)}), bf16[16,24,8192]{2,1,0:T(8,128)(2,1)}, u32[]{:S(2)}, u32[]{:S(2)}) %all-to-all-start) | async-done | bytes 6291488 | tf_op jit(solution)/shard_map/all_to_all | solution.py:45
  155.3 0.0 copy-start.1
  155.3 5.0 all-to-all-start.2
  160.3 0.0 copy-done.1
  160.3 4.8 fusion.11
  165.2 0.0 copy-done
  165.2 4.5 convolution_convert_fusion.1
  169.7 128.0 %all-to-all-done.2 = bf16[16,24,8192]{2,1,0:T(8,128)(2,1)} async-done(((bf16[16,24,8192]{2,1,0:T(8,128)(2,1)}), bf16[16,24,8192]{2,1,0:T(8,128)(2,1)}, u32[]{:S(2)}, u32[]{:S(2)}) %all-to-all-start.2) | async-done | bytes 6291488 | tf_op jit(solution)/shard_map/all_to_all | solution.py:52
  297.7 4.9 all-to-all-start.1
  302.7 4.8 fusion.7
  307.5 4.4 convolution_convert_fusion
  311.9 128.2 %all-to-all-done.1 = bf16[16,24,8192]{2,1,0:T(8,128)(2,1)} async-done(((bf16[16,24,8192]{2,1,0:T(8,128)(2,1)}), bf16[16,24,8192]{2,1,0:T(8,128)(2,1)}, u32[]{:S(2)}, u32[]{:S(2)}) %all-to-all-start.1) | async-done | bytes 6291488 | tf_op jit(solution)/shard_map/all_to_all | solution.py:64
  440.1 4.9 all-to-all-start.3
  445.0 5.0 fusion
  450.0 5.0 fusion.1
  455.0 8.7 %gather_fusion = bf16[128,8192]{1,0:T(8,128)(2,1)} fusion(bf16[384,8192]{1,0:T(8,128)(2,1)} %bitcast.8, s32[1024]{0:T(1024)S(1)} %pad_clamp_fusion), kind=kCustom, calls=%fused_computation | custom fusion | bytes 4194816 | tf_op jit(solution)/shard_map/gather | solution.py:79
  463.6 118.7 %all-to-all-done.3 = bf16[16,24,8192]{2,1,0:T(8,128)(2,1)} async-done(((bf16[16,24,8192]{2,1,0:T(8,128)(2,1)}), bf16[16,24,8192]{2,1,0:T(8,128)(2,1)}, u32[]{:S(2)}, u32[]{:S(2)}) %all-to-all-start.3) | async-done | bytes 6291488 | tf_op jit(solution)/shard_map/all_to_all | solution.py:71
  582.4 8.7 %gather_fusion.1 = bf16[128,8192]{1,0:T(8,128)(2,1)} fusion(bf16[384,8192]{1,0:T(8,128)(2,1)} %bitcast.12, s32[1024]{0:T(1024)S(1)} %pad_clamp_fusion), kind=kCustom, calls=%fused_computation.1 | custom fusion | bytes 4194816 | tf_op jit(solution)/shard_map/gather | solution.py:80
  (1 shorter events, 0.0 us)
Async XLA Ops:
  0.6 164.6 %copy-start = (bf16[1,64,8192]{2,1,0:T(8,128)(2,1)S(1)}, bf16[1,64,8192]{2,1,0:T(8,128)(2,1)}, u32[]{:S(2)}) copy-start(bf16[1,64,8192]{2,1,0:T(8,128)(2,1)} %param.9) | copy-start | bytes 3145732
  11.3 144.0 %all-to-all-start = ((bf16[16,24,8192]{2,1,0:T(8,128)(2,1)}), bf16[16,24,8192]{2,1,0:T(8,128)(2,1)}, u32[]{:S(2)}, u32[]{:S(2)}) async-start(bf16[16,24,8192]{2,1,0:T(8,128)(2,1)} %bitcast.40), calls=%async_computation | async-start | bytes 12582912 | tf_op jit(solution)/shard_map/all_to_all | solution.py:45
  155.3 5.0 copy-start.1
  155.3 142.4 %all-to-all-start.2 = ((bf16[16,24,8192]{2,1,0:T(8,128)(2,1)}), bf16[16,24,8192]{2,1,0:T(8,128)(2,1)}, u32[]{:S(2)}, u32[]{:S(2)}) async-start(bf16[16,24,8192]{2,1,0:T(8,128)(2,1)} %bitcast.39), calls=%async_computation.2 | async-start | bytes 12582912 | tf_op jit(solution)/shard_map/all_to_all | solution.py:52
  297.7 142.3 %all-to-all-start.1 = ((bf16[16,24,8192]{2,1,0:T(8,128)(2,1)}), bf16[16,24,8192]{2,1,0:T(8,128)(2,1)}, u32[]{:S(2)}, u32[]{:S(2)}) async-start(bf16[16,24,8192]{2,1,0:T(8,128)(2,1)} %bitcast.38), calls=%async_computation.1 | async-start | bytes 12582912 | tf_op jit(solution)/shard_map/all_to_all | solution.py:64
  440.1 142.3 %all-to-all-start.3 = ((bf16[16,24,8192]{2,1,0:T(8,128)(2,1)}), bf16[16,24,8192]{2,1,0:T(8,128)(2,1)}, u32[]{:S(2)}, u32[]{:S(2)}) async-start(bf16[16,24,8192]{2,1,0:T(8,128)(2,1)} %bitcast.37), calls=%async_computation.3 | async-start | bytes 12582912 | tf_op jit(solution)/shard_map/all_to_all | solution.py:71
where the time goes:
time: 592 us; the launch traced here: 591 us
  waiting for transfers between devices  504 us (85%)
  local copies, waits for them, and re-layouts  33.7 us (6%)
  matrix products  28.6 us (5%)
  starting transfers between devices  21.4 us (4%)
    all_to_all x1, waiting for transfers between devices, on_device(): lax.all_to_all(send_rows.reshape(owners, busy_cap, model_width), 'owner',...  129 us
    all_to_all x1, waiting for transfers between devices, on_device(): lax.all_to_all(result.reshape(owners, busy_cap, model_width), 'owner', sp...  128 us
    all_to_all x1, waiting for transfers between devices, on_device(): lax.all_to_all(send_cot.reshape(owners, busy_cap, model_width), 'owner',...  128 us
    all_to_all x1, waiting for transfers between devices, on_device(): lax.all_to_all(in_grad.reshape(owners, busy_cap, model_width), 'owner', s...  119 us
  transfers between devices with their start and end apart: 4, of which 4 were waited for; matrix products, arithmetic and copies ran while one was open for 8% of the time, Pallas kernels for 0%

commit v1 on v0

v1 whole, which is shorter than its diff:
```python
import jax
import jax.numpy as jnp
from jax import lax
from jax.sharding import PartitionSpec as P

BF = jnp.bfloat16
F32 = jnp.float32


def rows_by_rows(a, b):
    return lax.dot_general(a, b, (((1,), (1,)), ((), ())), preferred_element_type=F32)


def outer_sum(a, b):
    return lax.dot_general(a, b, (((0,), (0,)), ((), ())), preferred_element_type=F32)


def flip(x, bit, owners):
    return lax.ppermute(x, "owner", [(i, i ^ (1 << bit)) for i in range(owners)])


def halve(x, bit, me, owners, wire):
    half = x.shape[0] // 2
    mine = (me >> bit) & 1
    keep = lax.dynamic_slice_in_dim(x, mine * half, half, 0)
    give = lax.dynamic_slice_in_dim(x, (1 - mine) * half, half, 0)
    return keep + flip(give.astype(wire), bit, owners).astype(x.dtype)


def double(x, bit, me, owners):
    other = flip(x, bit, owners)
    mine = (me >> bit) & 1
    low = jnp.where(mine == 0, x, other)
    high = jnp.where(mine == 0, other, x)
    return jnp.concatenate([low, high], 0)


def line_sum(x, me, owners, inner, wire):
    length = owners // inner
    if length == 1:
        return x
    place = me // inner

    def hop(y, moves):
        pairs = [(a * inner + j, b * inner + j) for a, b in moves for j in range(inner)]
        return lax.ppermute(y.astype(wire), "owner", pairs).astype(x.dtype)

    mid = length // 2
    for s in range(mid - 1):
        x = x + hop(x, [(s, s + 1), (length - 1 - s, length - 2 - s)])
    x = x + hop(x, [(mid - 1, mid), (mid, mid - 1)])
    x = x.astype(wire).astype(x.dtype)
    for s in range(mid - 2, -1, -1):
        out = hop(x, [(s + 1, s), (length - 2 - s, length - 1 - s)])
        x = jnp.where((place == s) | (place == length - 1 - s), out, x)
    return x


def sum_over_owner(x, me, owners, wire):
    if owners & (owners - 1) or owners < 8:
        return lax.psum(x, "owner").astype(BF)
    x = halve(x, 0, me, owners, x.dtype)
    x = halve(x, 1, me, owners, wire)
    x = line_sum(x, me, owners, 4, wire).astype(BF)
    x = double(x, 1, me, owners)
    return double(x, 0, me, owners)


def exchange(x, owners):
    y = x.reshape(owners, x.shape[0] // owners, x.shape[1])
    y = lax.all_to_all(y, "owner", split_axis=0, concat_axis=0, tiled=True)
    return y.reshape(x.shape)


def gate(hidden, act_grad):
    sig = jax.nn.sigmoid(hidden)
    activated = (hidden * sig).astype(BF)
    hid_grad = (act_grad * sig * (1.0 + hidden * (1.0 - sig))).astype(BF)
    return activated, hid_grad


def on_device(tokens, task_ids, cotangent, down_factors, up_factors):
    owners = lax.axis_size("owner")
    me = lax.axis_index("owner")
    tok_count, width = tokens.shape
    cold_cap = tok_count // owners
    busy_cap = 3 * cold_cap
    cold_rows = owners * cold_cap
    down_mat = down_factors[0]
    up_mat = up_factors[0]
    rank = down_mat.shape[0]

    task_of = task_ids[:, 0]
    onehot = (task_of[:, None] == jnp.arange(owners, dtype=jnp.int32)[None, :]).astype(BF)
    earlier = jnp.tril(jnp.ones((tok_count, tok_count), BF), -1)
    before = jnp.dot(earlier, onehot, preferred_element_type=F32)
    rank_in = jnp.sum(before * onehot.astype(F32), axis=1).astype(jnp.int32)
    busy = jnp.argmax(jnp.sum(onehot.astype(F32), axis=0)).astype(jnp.int32)
    slot_of = jnp.where(task_of == busy, cold_rows + rank_in, task_of * cold_cap + rank_in)
    slots = jnp.arange(cold_rows + busy_cap, dtype=jnp.int32)
    place = (slots[:, None] == slot_of[None, :]).astype(BF)
    place_cold, place_busy = place[:cold_rows], place[cold_rows:]

    def pick(which, rows):
        return jnp.dot(which, rows, preferred_element_type=F32).astype(BF)

    got_rows = exchange(pick(place_cold, tokens), owners)
    got_cot = exchange(pick(place_cold, cotangent), owners)

    both = jnp.concatenate([down_mat, up_mat], 0)
    both = jnp.where(me == busy, both, jnp.zeros_like(both))
    both = sum_over_owner(both, me, owners, BF)
    busy_down, busy_up = both[:rank], both[rank:]
    busy_rows = pick(place_busy, tokens)
    busy_cot = pick(place_busy, cotangent)
    busy_act, busy_hid = gate(rows_by_rows(busy_rows, busy_down), rows_by_rows(busy_cot, busy_up))
    busy_sums = jnp.concatenate([outer_sum(busy_hid, busy_rows), outer_sum(busy_act, busy_cot)], 0)
    busy_sums = sum_over_owner(busy_sums, me, owners, BF)

    activated, hid_grad = gate(rows_by_rows(got_rows, down_mat), rows_by_rows(got_cot, up_mat))
    back_out = exchange(pick(activated, up_mat), owners)
    back_grad = exchange(pick(hid_grad, down_mat), owners)
    own_sums = jnp.concatenate([outer_sum(hid_grad, got_rows), outer_sum(activated, got_cot)], 0)
    sums = jnp.where(me == busy, busy_sums, own_sums.astype(BF))

    def put(cold, hot):
        cold = outer_sum(place_cold, cold)
        return (cold + outer_sum(place_busy, hot)).astype(BF)

    adapter_out = put(back_out, pick(busy_act, busy_up))
    input_grad = put(back_grad, pick(busy_hid, busy_down))
    return adapter_out, input_grad, sums[:rank][None], sums[rank:][None]


def solution(mesh):
    rows = P(("groups", "owner"), None)
    mats = P(("groups", "owner"), None, None)
    held = P("owner", None, None)
    return jax.shard_map(
        on_device,
        mesh=mesh,
        in_specs=(rows, rows, rows, held, held),
        out_specs=(rows, rows, mats, mats),
        check_vma=False,
    )
```

time: 592 us -> 334 us (0.56)
  waiting for transfers between devices: 504 us -> 219 us
  local copies, waits for them, and re-layouts: 33.7 us -> 5.75 us
  starting transfers between devices: 21.4 us -> 47.4 us
  other arithmetic: 2.49 us -> 22.2 us
  matrix products: 28.6 us -> 37.5 us
    all_to_all x4, waiting for transfers between devices: 504 us -> 71.9 us  [exchange(): y = lax.all_to_all(y, 'owner', split_axis=0, concat_axis=0, tiled=True)]
    ppermute x0 -> x14, waiting for transfers between devices: none -> 147 us  [the longest x6 89.9 us: hop(): return lax.ppermute(y.astype(wire), 'owner', pairs).astype(x.dtype)]
    ppermute x0 -> x14, starting transfers between devices: none -> 24.7 us  [the longest x6 12.4 us: hop(): return lax.ppermute(y.astype(wire), 'owner', pairs).astype(x.dtype)]
    gather x2 -> x0, local copies, waits for them, and re-layouts: 17.3 us -> none  [the longest x1 8.67 us: on_device(): input_grad = back_grad.reshape(-1, model_width)[slot_of]]
    scatter x2 -> x0, local copies, waits for them, and re-layouts: 16.3 us -> none  [the longest x1 8.18 us: on_device(): jnp.zeros((owners * busy_cap, model_width), tokens.dtype).at[slot_of]]
    dot_general x6 -> x19, matrix products: 28.6 us -> 37.5 us  [the longest x8 21.8 us: outer_sum(): lax.dot_general(a, b, (((0,), (0,)), ((), ())), preferred_element_type=F32)]
  transfers between devices with their start and end apart: 4 -> 18, of which waited for: 4 -> 13; matrix products, arithmetic and copies ran while one was open for 8% -> 14% of each run, Pallas kernels for 0% -> 0%
where the time goes in v1:
time: 334 us
  waiting for transfers between devices  219 us (66%)
  starting transfers between devices  47.4 us (14%)
  matrix products  37.5 us (11%)
  other arithmetic  22.2 us (7%)
  local copies, waits for them, and re-layouts  5.75 us (2%)
    ppermute x6, waiting for transfers between devices, hop(): return lax.ppermute(y.astype(wire), 'owner', pairs).astype(x.dtype)  89.9 us
    all_to_all x4, waiting for transfers between devices, exchange(): y = lax.all_to_all(y, 'owner', split_axis=0, concat_axis=0, tiled=True)  71.9 us
    ppermute x8, waiting for transfers between devices, flip(): return lax.ppermute(x, 'owner', [(i, i ^ 1 << bit) for i in range(owners)])  57.2 us
    all_to_all x4, starting transfers between devices, exchange(): y = lax.all_to_all(y, 'owner', split_axis=0, concat_axis=0, tiled=True)  22.7 us
    dot_general x8, matrix products, outer_sum(): lax.dot_general(a, b, (((0,), (0,)), ((), ())), preferred_element_type=F32)  21.8 us
    ppermute x6, starting transfers between devices, hop(): return lax.ppermute(y.astype(wire), 'owner', pairs).astype(x.dtype)  12.4 us
    ppermute x8, starting transfers between devices, flip(): return lax.ppermute(x, 'owner', [(i, i ^ 1 << bit) for i in range(owners)])  12.3 us
    dot_general x6, matrix products, pick(): return jnp.dot(which, rows, preferred_element_type=F32).astype(BF)  8.92 us
  transfers between devices with their start and end apart: 18, of which 13 were waited for; matrix products, arithmetic and copies ran while one was open for 14% of the time, Pallas kernels for 0%

profile of v1, /device:TPU:11, one launch (start us, length us, event | category | flops | bytes accessed | tf_op | source)
XLA Modules:
  0.0 333.5 jit_solution(5311250869414625281)
XLA Ops:
  7.0 2.4 collective-permute-done
  12.3 13.2 %collective-permute-done.1 = bf16[32,8192]{1,0:T(8,128)(2,1)} collective-permute-done((bf16[32,8192]{1,0:T(8,128)(2,1)}, bf16[32,8192]{1,0:T(8,128)(2,1)}, u32[]{:S(2)}, u32[]{:S(2)}) %collective-permute-start.1) | collective-permute-done | bytes 524320 | tf_op jit(solution)/shard_map/ppermute | solution.py:19
  28.0 12.8 %collective-permute-done.2 = bf16[32,8192]{1,0:T(8,128)(2,1)S(1)} collective-permute-done((bf16[32,8192]{1,0:T(8,128)(2,1)S(1)}, bf16[32,8192]{1,0:T(8,128)(2,1)S(1)}, u32[]{:S(2)}, u32[]{:S(2)}) %collective-permute-start.2) | collective-permute-done | bytes 524320 | tf_op jit(solution)/shard_map/ppermute | solution.py:46
  40.9 3.2 collective-permute-start.3
  44.2 10.0 %collective-permute-done.3 = bf16[32,8192]{1,0:T(8,128)(2,1)S(1)} collective-permute-done((bf16[32,8192]{1,0:T(8,128)(2,1)S(1)}, bf16[32,8192]{1,0:T(8,128)(2,1)S(1)}, u32[]{:S(2)}, u32[]{:S(2)}) %collective-permute-start.3) | collective-permute-done | bytes 524320 | tf_op jit(solution)/shard_map/ppermute | solution.py:46
  54.3 2.1 collective-permute-start.4
  56.4 7.6 %collective-permute-done.4 = bf16[32,8192]{1,0:T(8,128)(2,1)} collective-permute-done((bf16[32,8192]{1,0:T(8,128)(2,1)S(1)}, bf16[32,8192]{1,0:T(8,128)(2,1)}, u32[]{:S(2)}, u32[]{:S(2)}) %collective-permute-start.4) | collective-permute-done | bytes 524320 | tf_op jit(solution)/shard_map/ppermute | solution.py:46
  64.8 9.1 %collective-permute-done.5 = bf16[32,8192]{1,0:T(8,128)(2,1)} collective-permute-done((bf16[32,8192]{1,0:T(8,128)(2,1)S(1)}, bf16[32,8192]{1,0:T(8,128)(2,1)}, u32[]{:S(2)}, u32[]{:S(2)}) %collective-permute-start.5) | collective-permute-done | bytes 524320 | tf_op jit(solution)/shard_map/ppermute | solution.py:19
  76.4 4.6 %collective-permute-start.6 = (bf16[64,8192]{1,0:T(8,128)(2,1)}, bf16[64,8192]{1,0:T(8,128)(2,1)}, u32[]{:S(2)}, u32[]{:S(2)}) collective-permute-start(bf16[64,8192]{1,0:T(8,128)(2,1)} %pad_maximum_fusion), channel_id=1, source_target_pairs={{0,1},{1,0},{2,3},{3,2},{4,5},{5,4},{6,7},{7,6},{8,9},{9,8},{10,11... | collective-permute-start | bytes 3145736 | tf_op jit(solution)/shard_map/ppermute | solution.py:19
  83.7 8.0 %all-to-all-start = ((bf16[16,8,8192]{2,1,0:T(8,128)(2,1)}), bf16[16,8,8192]{2,1,0:T(8,128)(2,1)}, u32[]{:S(2)}, u32[]{:S(2)}) async-start(bf16[16,8,8192]{2,1,0:T(8,128)(2,1)} %fusion.2), calls=%async_computation | async-start | bytes 4194304 | tf_op jit(solution)/shard_map/all_to_all | solution.py:71
  96.8 2.2 fusion.6
  101.5 37.8 %all-to-all-done = bf16[16,8,8192]{2,1,0:T(8,128)(2,1)} async-done(((bf16[16,8,8192]{2,1,0:T(8,128)(2,1)}), bf16[16,8,8192]{2,1,0:T(8,128)(2,1)}, u32[]{:S(2)}, u32[]{:S(2)}) %all-to-all-start) | async-done | bytes 2097184 | tf_op jit(solution)/shard_map/all_to_all | solution.py:71
  139.3 4.9 %all-to-all-start.2 = ((bf16[16,8,8192]{2,1,0:T(8,128)(2,1)}), bf16[16,8,8192]{2,1,0:T(8,128)(2,1)S(1)}, u32[]{:S(2)}, u32[]{:S(2)}) async-start(bf16[16,8,8192]{2,1,0:T(8,128)(2,1)} %fusion.3), calls=%async_computation.2 | async-start | bytes 4194304 | tf_op jit(solution)/shard_map/all_to_all | solution.py:71
  144.2 2.5 fusion.8
  147.2 23.5 %collective-permute-done.8 = bf16[32,8192]{1,0:T(8,128)(2,1)S(1)} collective-permute-done((bf16[32,8192]{1,0:T(8,128)(2,1)S(1)}, bf16[32,8192]{1,0:T(8,128)(2,1)S(1)}, u32[]{:S(2)}, u32[]{:S(2)}) %collective-permute-start.8) | collective-permute-done | bytes 524320 | tf_op jit(solution)/shard_map/ppermute | solution.py:19
  173.0 2.4 fusion.17
  175.5 16.3 %all-to-all-done.2 = bf16[16,8,8192]{2,1,0:T(8,128)(2,1)S(1)} async-done(((bf16[16,8,8192]{2,1,0:T(8,128)(2,1)}), bf16[16,8,8192]{2,1,0:T(8,128)(2,1)S(1)}, u32[]{:S(2)}, u32[]{:S(2)}) %all-to-all-start.2) | async-done | bytes 2097184 | tf_op jit(solution)/shard_map/all_to_all | solution.py:71
  195.8 5.0 %all-to-all-start.3 = ((bf16[16,8,8192]{2,1,0:T(8,128)(2,1)}), bf16[16,8,8192]{2,1,0:T(8,128)(2,1)}, u32[]{:S(2)}, u32[]{:S(2)}) async-start(bf16[16,8,8192]{2,1,0:T(8,128)(2,1)} %fusion.5), calls=%async_computation.3 | async-start | bytes 4194304 | tf_op jit(solution)/shard_map/all_to_all | solution.py:71
  202.6 3.2 collective-permute-start.10
  205.8 53.5 %collective-permute-done.10 = bf16[32,8192]{1,0:T(8,128)(2,1)S(1)} collective-permute-done((bf16[32,8192]{1,0:T(8,128)(2,1)S(1)}, bf16[32,8192]{1,0:T(8,128)(2,1)S(1)}, u32[]{:S(2)}, u32[]{:S(2)}) %collective-permute-start.10) | collective-permute-done | bytes 524320 | tf_op jit(solution)/shard_map/ppermute | solution.py:46
  262.0 2.1 fusion.4
  265.5 4.7 %all-to-all-start.1 = ((bf16[16,8,8192]{2,1,0:T(8,128)(2,1)}), bf16[16,8,8192]{2,1,0:T(8,128)(2,1)S(1)}, u32[]{:S(2)}, u32[]{:S(2)}) async-start(bf16[16,8,8192]{2,1,0:T(8,128)(2,1)} %fusion.4), calls=%async_computation.1 | async-start | bytes 4194304 | tf_op jit(solution)/shard_map/all_to_all | solution.py:71
  270.2 6.0 %collective-permute-done.11 = bf16[32,8192]{1,0:T(8,128)(2,1)S(1)} collective-permute-done((bf16[32,8192]{1,0:T(8,128)(2,1)S(1)}, bf16[32,8192]{1,0:T(8,128)(2,1)S(1)}, u32[]{:S(2)}, u32[]{:S(2)}) %collective-permute-start.11) | collective-permute-done | bytes 524320 | tf_op jit(solution)/shard_map/ppermute | solution.py:46
  276.3 3.1 collective-permute-start.12
  279.4 3.1 convolution_convert_fusion.5
  282.4 4.3 %fusion.9 = f32[128,8192]{1,0:T(8,128)} fusion(bf16[16,8,8192]{2,1,0:T(8,128)(2,1)} %all-to-all-done.3, pred[152,128]{1,0:T(8,128)(4,1)S(1)} %iota_compare_fusion), kind=kOutput, calls=%fused_computation.27 | convolution fusion | flops 268435456 | bytes 6307840 | tf_op jit(solution)/shard_map/dot_general | solution.py:15
  286.8 8.9 %collective-permute-done.12 = bf16[32,8192]{1,0:T(8,128)(2,1)S(1)} collective-permute-done((bf16[32,8192]{1,0:T(8,128)(2,1)S(1)}, bf16[32,8192]{1,0:T(8,128)(2,1)S(1)}, u32[]{:S(2)}, u32[]{:S(2)}) %collective-permute-start.12) | collective-permute-done | bytes 524320 | tf_op jit(solution)/shard_map/ppermute | solution.py:19
  297.1 2.6 collective-permute-start.13
  299.7 17.9 %all-to-all-done.1 = bf16[16,8,8192]{2,1,0:T(8,128)(2,1)S(1)} async-done(((bf16[16,8,8192]{2,1,0:T(8,128)(2,1)}), bf16[16,8,8192]{2,1,0:T(8,128)(2,1)S(1)}, u32[]{:S(2)}, u32[]{:S(2)}) %all-to-all-start.1) | async-done | bytes 2097184 | tf_op jit(solution)/shard_map/all_to_all | solution.py:71
  317.6 2.8 fusion.14
  320.4 4.7 %fusion.1 = bf16[128,8192]{1,0:T(8,128)(2,1)} fusion(f32[128,8192]{1,0:T(8,128)} %fusion.9, bf16[24,64]{1,0:T(8,128)(2,1)S(1)} %fusion.29, bf16[64,8192]{1,0:T(8,128)(2,1)} %collective-permute-done.6, pred[]{:T(512)S(6)} %eq.70, pred[152,128]{1,0:T(8,128)(4,1)S(1)} %iota_compare_fusion, bf16[32,8192]{1,0:T(8,128)(2,1)S(1)} %copy-done.13, ...), kind=kOutput, calls=%fused_computation.3 | convolution fusion | flops 80412672 | bytes 8397825 | tf_op jit(solution)/shard_map/dot_general | solution.py:15
  325.1 4.5 %fusion = bf16[128,8192]{1,0:T(8,128)(2,1)} fusion(f32[128,8192]{1,0:T(8,128)} %fusion.14, bf16[64,8192]{1,0:T(8,128)(2,1)} %collective-permute-done.6, pred[]{:T(512)S(6)} %eq.70, pred[152,128]{1,0:T(8,128)(4,1)S(1)} %iota_compare_fusion, f32[24,64]{1,0:T(8,128)S(1)} %fusion.32, bf16[32,8192]{1,0:T(8,128)(2,1)S(1)} %copy-done.13, ...), kind=kOutput, calls=%fused_computation.2 | convolution fusion | flops 80420352 | bytes 8403969 | tf_op jit(solution)/shard_map/dot_general | solution.py:15
  (98 shorter events, 42.7 us)
Async XLA Ops:
  0.6 81.1 %copy-start = (bf16[128,8192]{1,0:T(8,128)(2,1)S(1)}, bf16[128,8192]{1,0:T(8,128)(2,1)}, u32[]{:S(2)}) copy-start(bf16[128,8192]{1,0:T(8,128)(2,1)} %param.5) | copy-start | bytes 6291460
  6.3 3.2 collective-permute-start
  12.1 13.5 %collective-permute-start.1 = (bf16[32,8192]{1,0:T(8,128)(2,1)}, bf16[32,8192]{1,0:T(8,128)(2,1)}, u32[]{:S(2)}, u32[]{:S(2)}) collective-permute-start(bf16[32,8192]{1,0:T(8,128)(2,1)} %constant_dynamic-slice_fusion), channel_id=1, source_target_pairs={{0,2},{1,3},{2,0},{3,1},{4,6},{5,7},{6,4},{7,5},{8,10},{9,11},{10,... | collective-permute-start | bytes 1572872 | tf_op jit(solution)/shard_map/ppermute | solution.py:19
  26.7 37.7 %copy-start.23 = (s32[128,1]{0,1:T(1,128)S(1)}, s32[128,1]{0,1:T(1,128)}, u32[]{:S(2)}) copy-start(s32[128,1]{0,1:T(1,128)} %param.6) | copy-start | bytes 1540
  26.7 14.1 %collective-permute-start.2 = (bf16[32,8192]{1,0:T(8,128)(2,1)S(1)}, bf16[32,8192]{1,0:T(8,128)(2,1)S(1)}, u32[]{:S(2)}, u32[]{:S(2)}) collective-permute-start(bf16[32,8192]{1,0:T(8,128)(2,1)S(1)} %dynamic-slice_add_fusion.1), channel_id=1, source_target_pairs={{0,4},{1,5},{2,6},{3,7},{12,8},{13,9},{14,10},{15,11},{16,20},{17,... | collective-permute-start | bytes 1572872 | tf_op jit(solution)/shard_map/ppermute | solution.py:46
  40.9 13.2 %collective-permute-start.3 = (bf16[32,8192]{1,0:T(8,128)(2,1)S(1)}, bf16[32,8192]{1,0:T(8,128)(2,1)S(1)}, u32[]{:S(2)}, u32[]{:S(2)}) collective-permute-start(bf16[32,8192]{1,0:T(8,128)(2,1)S(1)} %add.97), channel_id=1, source_target_pairs={{4,8},{5,9},{6,10},{7,11},{8,4},{9,5},{10,6},{11,7},{20,24},{21,25... | collective-permute-start | bytes 1572872 | tf_op jit(solution)/shard_map/ppermute | solution.py:46
  54.3 9.7 %collective-permute-start.4 = (bf16[32,8192]{1,0:T(8,128)(2,1)S(1)}, bf16[32,8192]{1,0:T(8,128)(2,1)}, u32[]{:S(2)}, u32[]{:S(2)}) collective-permute-start(bf16[32,8192]{1,0:T(8,128)(2,1)S(1)} %add.98), channel_id=1, source_target_pairs={{4,0},{5,1},{6,2},{7,3},{8,12},{9,13},{10,14},{11,15},{20,16},{21,... | collective-permute-start | bytes 1572872 | tf_op jit(solution)/shard_map/ppermute | solution.py:46
  64.1 9.9 %collective-permute-start.5 = (bf16[32,8192]{1,0:T(8,128)(2,1)S(1)}, bf16[32,8192]{1,0:T(8,128)(2,1)}, u32[]{:S(2)}, u32[]{:S(2)}) collective-permute-start(bf16[32,8192]{1,0:T(8,128)(2,1)S(1)} %broadcast_select_fusion.4), channel_id=1, source_target_pairs={{0,2},{1,3},{2,0},{3,1},{4,6},{5,7},{6,4},{7,5},{8,10},{9,11},{10,... | collective-permute-start | bytes 1572872 | tf_op jit(solution)/shard_map/ppermute | solution.py:19
  75.2 20.2 %copy-start.10 = (bf16[32,8192]{1,0:T(8,128)(2,1)}, bf16[32,8192]{1,0:T(8,128)(2,1)S(1)}, u32[]{:S(2)}) copy-start(bf16[32,8192]{1,0:T(8,128)(2,1)S(1)} %get-tuple-element.12) | copy-start | bytes 1572868
  75.2 20.2 %copy-start.12 = (bf16[32,8192]{1,0:T(8,128)(2,1)}, bf16[32,8192]{1,0:T(8,128)(2,1)S(1)}, u32[]{:S(2)}) copy-start(bf16[32,8192]{1,0:T(8,128)(2,1)S(1)} %get-tuple-element.13) | copy-start | bytes 1572868
  76.4 17.3 %collective-permute-start.6 = (bf16[64,8192]{1,0:T(8,128)(2,1)}, bf16[64,8192]{1,0:T(8,128)(2,1)}, u32[]{:S(2)}, u32[]{:S(2)}) collective-permute-start(bf16[64,8192]{1,0:T(8,128)(2,1)} %pad_maximum_fusion), channel_id=1, source_target_pairs={{0,1},{1,0},{2,3},{3,2},{4,5},{5,4},{6,7},{7,6},{8,9},{9,8},{10,11... | collective-permute-start | bytes 3145736 | tf_op jit(solution)/shard_map/ppermute | solution.py:19
  83.7 55.6 %all-to-all-start = ((bf16[16,8,8192]{2,1,0:T(8,128)(2,1)}), bf16[16,8,8192]{2,1,0:T(8,128)(2,1)}, u32[]{:S(2)}, u32[]{:S(2)}) async-start(bf16[16,8,8192]{2,1,0:T(8,128)(2,1)} %fusion.2), calls=%async_computation | async-start | bytes 4194304 | tf_op jit(solution)/shard_map/all_to_all | solution.py:71
  96.3 2.7 copy-start.2
  99.1 45.1 %collective-permute-start.7 = (f32[64,8192]{1,0:T(8,128)}, f32[64,8192]{1,0:T(8,128)}, u32[]{:S(2)}, u32[]{:S(2)}) collective-permute-start(f32[64,8192]{1,0:T(8,128)} %fusion.6), channel_id=1, source_target_pairs={{0,1},{1,0},{2,3},{3,2},{4,5},{5,4},{6,7},{7,6},{8,9},{9,8},{10,11... | collective-permute-start | bytes 6291464 | tf_op jit(solution)/shard_map/ppermute | solution.py:19
  139.3 52.4 %all-to-all-start.2 = ((bf16[16,8,8192]{2,1,0:T(8,128)(2,1)}), bf16[16,8,8192]{2,1,0:T(8,128)(2,1)S(1)}, u32[]{:S(2)}, u32[]{:S(2)}) async-start(bf16[16,8,8192]{2,1,0:T(8,128)(2,1)} %fusion.3), calls=%async_computation.2 | async-start | bytes 4194304 | tf_op jit(solution)/shard_map/all_to_all | solution.py:71
  146.8 26.2 %copy-start.4 = (f32[64,8192]{1,0:T(8,128)}, f32[64,8192]{1,0:T(8,128)S(1)}, u32[]{:S(2)}) copy-start(f32[64,8192]{1,0:T(8,128)S(1)} %fusion.8) | copy-start | bytes 6291460
  146.8 26.2 %copy-start.6 = (bf16[1,64,8192]{2,1,0:T(8,128)(2,1)S(1)}, bf16[1,64,8192]{2,1,0:T(8,128)(2,1)}, u32[]{:S(2)}) copy-start(bf16[1,64,8192]{2,1,0:T(8,128)(2,1)} %param.8) | copy-start | bytes 3145732
  146.9 23.9 %collective-permute-start.8 = (bf16[32,8192]{1,0:T(8,128)(2,1)S(1)}, bf16[32,8192]{1,0:T(8,128)(2,1)S(1)}, u32[]{:S(2)}, u32[]{:S(2)}) collective-permute-start(bf16[32,8192]{1,0:T(8,128)(2,1)S(1)} %dynamic-slice_convert_fusion), channel_id=1, source_target_pairs={{0,2},{1,3},{2,0},{3,1},{4,6},{5,7},{6,4},{7,5},{8,10},{9,11},{10,... | collective-permute-start | bytes 1572872 | tf_op jit(solution)/shard_map/ppermute | solution.py:19
  171.7 29.2 %collective-permute-start.9 = (bf16[32,8192]{1,0:T(8,128)(2,1)}, bf16[32,8192]{1,0:T(8,128)(2,1)}, u32[]{:S(2)}, u32[]{:S(2)}) collective-permute-start(bf16[32,8192]{1,0:T(8,128)(2,1)} %fusion.33), channel_id=1, source_target_pairs={{0,4},{1,5},{2,6},{3,7},{12,8},{13,9},{14,10},{15,11},{16,20},{17,... | collective-permute-start | bytes 1572872 | tf_op jit(solution)/shard_map/ppermute | solution.py:46
  195.8 5.1 %copy-start.19 = (bf16[32,8192]{1,0:T(8,128)(2,1)S(1)}, bf16[32,8192]{1,0:T(8,128)(2,1)}, u32[]{:S(2)}) copy-start(bf16[32,8192]{1,0:T(8,128)(2,1)} %copy-done.18) | copy-start | bytes 1572868
  195.8 69.6 %all-to-all-start.3 = ((bf16[16,8,8192]{2,1,0:T(8,128)(2,1)}), bf16[16,8,8192]{2,1,0:T(8,128)(2,1)}, u32[]{:S(2)}, u32[]{:S(2)}) async-start(bf16[16,8,8192]{2,1,0:T(8,128)(2,1)} %fusion.5), calls=%async_computation.3 | async-start | bytes 4194304 | tf_op jit(solution)/shard_map/all_to_all | solution.py:71
  200.9 58.5 %copy-start.5 = (f32[64,8192]{1,0:T(8,128)S(1)}, f32[64,8192]{1,0:T(8,128)}, u32[]{:S(2)}) copy-start(f32[64,8192]{1,0:T(8,128)} %copy-done.4) | copy-start | bytes 6291460
  202.6 59.4 %copy-start.7 = (bf16[1,64,8192]{2,1,0:T(8,128)(2,1)S(1)}, bf16[1,64,8192]{2,1,0:T(8,128)(2,1)}, u32[]{:S(2)}) copy-start(bf16[1,64,8192]{2,1,0:T(8,128)(2,1)} %param.9) | copy-start | bytes 3145732
  202.6 56.7 %collective-permute-start.10 = (bf16[32,8192]{1,0:T(8,128)(2,1)S(1)}, bf16[32,8192]{1,0:T(8,128)(2,1)S(1)}, u32[]{:S(2)}, u32[]{:S(2)}) collective-permute-start(bf16[32,8192]{1,0:T(8,128)(2,1)S(1)} %fusion.31), channel_id=1, source_target_pairs={{4,8},{5,9},{6,10},{7,11},{8,4},{9,5},{10,6},{11,7},{20,24},{21,25... | collective-permute-start | bytes 1572872 | tf_op jit(solution)/shard_map/ppermute | solution.py:46
  260.6 15.6 %collective-permute-start.11 = (bf16[32,8192]{1,0:T(8,128)(2,1)S(1)}, bf16[32,8192]{1,0:T(8,128)(2,1)S(1)}, u32[]{:S(2)}, u32[]{:S(2)}) collective-permute-start(bf16[32,8192]{1,0:T(8,128)(2,1)S(1)} %add_convert_fusion), channel_id=1, source_target_pairs={{4,0},{5,1},{6,2},{7,3},{8,12},{9,13},{10,14},{11,15},{20,16},{21,... | collective-permute-start | bytes 1572872 | tf_op jit(solution)/shard_map/ppermute | solution.py:46
  265.5 52.1 %all-to-all-start.1 = ((bf16[16,8,8192]{2,1,0:T(8,128)(2,1)}), bf16[16,8,8192]{2,1,0:T(8,128)(2,1)S(1)}, u32[]{:S(2)}, u32[]{:S(2)}) async-start(bf16[16,8,8192]{2,1,0:T(8,128)(2,1)} %fusion.4), calls=%async_computation.1 | async-start | bytes 4194304 | tf_op jit(solution)/shard_map/all_to_all | solution.py:71
  276.3 19.3 %collective-permute-start.12 = (bf16[32,8192]{1,0:T(8,128)(2,1)S(1)}, bf16[32,8192]{1,0:T(8,128)(2,1)S(1)}, u32[]{:S(2)}, u32[]{:S(2)}) collective-permute-start(bf16[32,8192]{1,0:T(8,128)(2,1)S(1)} %select_convert_fusion), channel_id=1, source_target_pairs={{0,2},{1,3},{2,0},{3,1},{4,6},{5,7},{6,4},{7,5},{8,10},{9,11},{10,... | collective-permute-start | bytes 1572872 | tf_op jit(solution)/shard_map/ppermute | solution.py:19
  297.1 23.2 %copy-start.11 = (bf16[32,8192]{1,0:T(8,128)(2,1)S(1)}, bf16[32,8192]{1,0:T(8,128)(2,1)}, u32[]{:S(2)}) copy-start(bf16[32,8192]{1,0:T(8,128)(2,1)} %copy-done.10) | copy-start | bytes 1572868
  297.1 23.2 %copy-start.13 = (bf16[32,8192]{1,0:T(8,128)(2,1)S(1)}, bf16[32,8192]{1,0:T(8,128)(2,1)}, u32[]{:S(2)}) copy-start(bf16[32,8192]{1,0:T(8,128)(2,1)} %copy-done.12) | copy-start | bytes 1572868
  297.1 32.5 %collective-permute-start.13 = (bf16[64,8192]{1,0:T(8,128)(2,1)}, bf16[64,8192]{1,0:T(8,128)(2,1)}, u32[]{:S(2)}, u32[]{:S(2)}) collective-permute-start(bf16[64,8192]{1,0:T(8,128)(2,1)} %pad_maximum_fusion.1), channel_id=1, source_target_pairs={{0,1},{1,0},{2,3},{3,2},{4,5},{5,4},{6,7},{7,6},{8,9},{9,8},{10,11... | collective-permute-start | bytes 3145736 | tf_op jit(solution)/shard_map/ppermute | solution.py:19
  325.1 4.5 %copy-start.15 = (bf16[32,8192]{1,0:T(8,128)(2,1)S(1)}, bf16[32,8192]{1,0:T(8,128)(2,1)}, u32[]{:S(2)}) copy-start(bf16[32,8192]{1,0:T(8,128)(2,1)} %copy-done.14) | copy-start | bytes 1572868
  325.1 4.5 %copy-start.17 = (bf16[32,8192]{1,0:T(8,128)(2,1)S(1)}, bf16[32,8192]{1,0:T(8,128)(2,1)}, u32[]{:S(2)}) copy-start(bf16[32,8192]{1,0:T(8,128)(2,1)} %copy-done.16) | copy-start | bytes 1572868
  (10 other events, 16.5 us)

commit v2 on v1

--- a/solution.py
+++ b/solution.py
@@ -35,7 +35,11 @@
     return jnp.concatenate([low, high], 0)
 
 
-def line_sum(x, me, owners, inner, wire):
+def after(x, other):
+    return x + jnp.minimum(jnp.abs(other[0, 0].astype(F32)), 0.0).astype(x.dtype)
+
+
+def line_sum(x, me, owners, inner, wire, first):
     length = owners // inner
     if length == 1:
         return x
@@ -48,6 +52,7 @@
     mid = length // 2
     for s in range(mid - 1):
         x = x + hop(x, [(s, s + 1), (length - 1 - s, length - 2 - s)])
+    x = after(x, first)
     x = x + hop(x, [(mid - 1, mid), (mid, mid - 1)])
     x = x.astype(wire).astype(x.dtype)
     for s in range(mid - 2, -1, -1):
@@ -56,14 +61,15 @@
     return x
 
 
-def sum_over_owner(x, me, owners, wire):
+def sum_over_owner(x, me, owners, wire, ties):
     if owners & (owners - 1) or owners < 8:
         return lax.psum(x, "owner").astype(BF)
-    x = halve(x, 0, me, owners, x.dtype)
+    middle, third, last = ties
+    x = halve(x, 0, me, owners, wire)
     x = halve(x, 1, me, owners, wire)
-    x = line_sum(x, me, owners, 4, wire).astype(BF)
-    x = double(x, 1, me, owners)
-    return double(x, 0, me, owners)
+    x = line_sum(x, me, owners, 4, wire, middle).astype(BF)
+    x = double(after(x, third), 1, me, owners)
+    return double(after(x, last), 0, me, owners)
 
 
 def exchange(x, owners):
@@ -107,21 +113,19 @@
     got_rows = exchange(pick(place_cold, tokens), owners)
     got_cot = exchange(pick(place_cold, cotangent), owners)
 
+    activated, hid_grad = gate(rows_by_rows(got_rows, down_mat), rows_by_rows(got_cot, up_mat))
+    back_out = exchange(pick(activated, up_mat), owners)
+    back_grad = exchange(pick(hid_grad, down_mat), owners)
+    own_sums = jnp.concatenate([outer_sum(hid_grad, got_rows), outer_sum(activated, got_cot)], 0)
+
     both = jnp.concatenate([down_mat, up_mat], 0)
     both = jnp.where(me == busy, both, jnp.zeros_like(both))
-    both = sum_over_owner(both, me, owners, BF)
+    both = sum_over_owner(both, me, owners, BF, (got_rows, got_cot, back_out))
     busy_down, busy_up = both[:rank], both[rank:]
     busy_rows = pick(place_busy, tokens)
     busy_cot = pick(place_busy, cotangent)
     busy_act, busy_hid = gate(rows_by_rows(busy_rows, busy_down), rows_by_rows(busy_cot, busy_up))
     busy_sums = jnp.concatenate([outer_sum(busy_hid, busy_rows), outer_sum(busy_act, busy_cot)], 0)
-    busy_sums = sum_over_owner(busy_sums, me, owners, BF)
-
-    activated, hid_grad = gate(rows_by_rows(got_rows, down_mat), rows_by_rows(got_cot, up_mat))
-    back_out = exchange(pick(activated, up_mat), owners)
-    back_grad = exchange(pick(hid_grad, down_mat), owners)
-    own_sums = jnp.concatenate([outer_sum(hid_grad, got_rows), outer_sum(activated, got_cot)], 0)
-    sums = jnp.where(me == busy, busy_sums, own_sums.astype(BF))
 
     def put(cold, hot):
         cold = outer_sum(place_cold, cold)
@@ -129,6 +133,8 @@
 
     adapter_out = put(back_out, pick(busy_act, busy_up))
     input_grad = put(back_grad, pick(busy_hid, busy_down))
+    busy_sums = sum_over_owner(busy_sums, me, owners, BF, (back_grad, adapter_out, input_grad))
+    sums = jnp.where(me == busy, busy_sums, own_sums.astype(BF))
     return adapter_out, input_grad, sums[:rank][None], sums[rank:][None]
 
 

time: 334 us -> 323 us (0.967)
  waiting for transfers between devices: 219 us -> 202 us
  starting transfers between devices: 47.4 us -> 39.8 us
  local copies, waits for them, and re-layouts: 5.75 us -> 12.9 us
  between operations: 1.71 us -> 5.66 us
    ppermute x6, waiting for transfers between devices: 89.9 us -> 69.3 us  [hop(): return lax.ppermute(y.astype(wire), 'owner', pairs).astype(x.dtype)]
    all_to_all x4, waiting for transfers between devices: 71.9 us -> 80.8 us  [exchange(): y = lax.all_to_all(y, 'owner', split_axis=0, concat_axis=0, tiled=True)]
    ppermute x8, starting transfers between devices: 12.3 us -> 4.5 us  [flip(): return lax.ppermute(x, 'owner', [(i, i ^ 1 << bit) for i in range(owners)])]
    slice x0 -> x6, local copies, waits for them, and re-layouts: none -> 6.56 us  [after(): other[0, 0].astype(F32)]
    ppermute x8, waiting for transfers between devices: 57.2 us -> 51.7 us  [flip(): return lax.ppermute(x, 'owner', [(i, i ^ 1 << bit) for i in range(owners)])]
    concatenate x3 -> x0, other arithmetic: 4.47 us -> none  [the longest x2 2.29 us: double(): return jnp.concatenate([low, high], 0)]
    add x1 -> x5, other arithmetic: 0.12 us -> 4.07 us  [after(): x + jnp.minimum(jnp.abs(other[0, 0].astype(F32)), 0.0).astype(x.dtype)]
  transfers between devices with their start and end apart: 18 -> 18, of which waited for: 13 -> 11; matrix products, arithmetic and copies ran while one was open for 14% -> 16% of each run, Pallas kernels for 0% -> 0%
where the time goes in v2:
time: 323 us; the launch traced here: 319 us
  waiting for transfers between devices  202 us (63%)
  starting transfers between devices  39.8 us (12%)
  matrix products  37.7 us (12%)
  other arithmetic  21.6 us (7%)
  local copies, waits for them, and re-layouts  12.9 us (4%)
  between operations  5.66 us (2%)
    all_to_all x4, waiting for transfers between devices, exchange(): y = lax.all_to_all(y, 'owner', split_axis=0, concat_axis=0, tiled=True)  80.8 us
    ppermute x6, waiting for transfers between devices, hop(): return lax.ppermute(y.astype(wire), 'owner', pairs).astype(x.dtype)  69.3 us
    ppermute x8, waiting for transfers between devices, flip(): return lax.ppermute(x, 'owner', [(i, i ^ 1 << bit) for i in range(owners)])  51.7 us
    all_to_all x4, starting transfers between devices, exchange(): y = lax.all_to_all(y, 'owner', split_axis=0, concat_axis=0, tiled=True)  22.7 us
    dot_general x8, matrix products, outer_sum(): lax.dot_general(a, b, (((0,), (0,)), ((), ())), preferred_element_type=F32)  21.3 us
    ppermute x6, starting transfers between devices, hop(): return lax.ppermute(y.astype(wire), 'owner', pairs).astype(x.dtype)  12.6 us
    dot_general x6, matrix products, pick(): return jnp.dot(which, rows, preferred_element_type=F32).astype(BF)  8.92 us
    dot_general x4, matrix products, rows_by_rows(): lax.dot_general(a, b, (((1,), (1,)), ((), ())), preferred_element_type=F32)  7.19 us
  transfers between devices with their start and end apart: 18, of which 11 were waited for; matrix products, arithmetic and copies ran while one was open for 16% of the time, Pallas kernels for 0%

profile of v2, /device:TPU:11, one launch (start us, length us, event | category | flops | bytes accessed | tf_op | source)
XLA Modules:
  0.0 319.4 jit_solution(3497488573299801309)
XLA Ops:
  2.9 2.0 maximum_select_fusion
  8.0 2.0 fusion.2
  10.0 6.4 %all-to-all-start = ((bf16[16,8,8192]{2,1,0:T(8,128)(2,1)}), bf16[16,8,8192]{2,1,0:T(8,128)(2,1)}, u32[]{:S(2)}, u32[]{:S(2)}) async-start(bf16[16,8,8192]{2,1,0:T(8,128)(2,1)} %fusion.2), calls=%async_computation | async-start | bytes 4194304 | tf_op jit(solution)/shard_map/all_to_all | solution.py:77
  16.4 1.8 dynamic-slice_add_fusion
  19.3 2.0 fusion.3
  21.3 42.7 %all-to-all-done = bf16[16,8,8192]{2,1,0:T(8,128)(2,1)} async-done(((bf16[16,8,8192]{2,1,0:T(8,128)(2,1)}), bf16[16,8,8192]{2,1,0:T(8,128)(2,1)}, u32[]{:S(2)}, u32[]{:S(2)}) %all-to-all-start) | async-done | bytes 2097184 | tf_op jit(solution)/shard_map/all_to_all | solution.py:77
  64.0 4.9 %all-to-all-start.2 = ((bf16[16,8,8192]{2,1,0:T(8,128)(2,1)}), bf16[16,8,8192]{2,1,0:T(8,128)(2,1)}, u32[]{:S(2)}, u32[]{:S(2)}) async-start(bf16[16,8,8192]{2,1,0:T(8,128)(2,1)} %fusion.3), calls=%async_computation.2 | async-start | bytes 4194304 | tf_op jit(solution)/shard_map/all_to_all | solution.py:77
  73.3 42.5 %collective-permute-done.2 = bf16[32,8192]{1,0:T(8,128)(2,1)S(1)} collective-permute-done((bf16[32,8192]{1,0:T(8,128)(2,1)S(1)}, bf16[32,8192]{1,0:T(8,128)(2,1)S(1)}, u32[]{:S(2)}, u32[]{:S(2)}) %collective-permute-start.2) | collective-permute-done | bytes 524320 | tf_op jit(solution)/shard_map/ppermute | solution.py:50
  115.8 3.8 %collective-permute-start.3 = (bf16[32,8192]{1,0:T(8,128)(2,1)S(1)}, bf16[32,8192]{1,0:T(8,128)(2,1)S(1)}, u32[]{:S(2)}, u32[]{:S(2)}) collective-permute-start(bf16[32,8192]{1,0:T(8,128)(2,1)S(1)} %add_add_fusion.1), channel_id=1, source_target_pairs={{4,8},{5,9},{6,10},{7,11},{8,4},{9,5},{10,6},{11,7},{20,24},{21,25... | collective-permute-start | bytes 1572872 | tf_op jit(solution)/shard_map/ppermute | solution.py:50
  119.6 11.4 %collective-permute-done.3 = bf16[32,8192]{1,0:T(8,128)(2,1)S(1)} collective-permute-done((bf16[32,8192]{1,0:T(8,128)(2,1)S(1)}, bf16[32,8192]{1,0:T(8,128)(2,1)S(1)}, u32[]{:S(2)}, u32[]{:S(2)}) %collective-permute-start.3) | collective-permute-done | bytes 524320 | tf_op jit(solution)/shard_map/ppermute | solution.py:50
  131.9 2.1 collective-permute-start.4
  135.9 2.7 fusion.43
  138.6 2.1 fusion.4
  140.7 6.5 %all-to-all-start.1 = ((bf16[16,8,8192]{2,1,0:T(8,128)(2,1)}), bf16[16,8,8192]{2,1,0:T(8,128)(2,1)}, u32[]{:S(2)}, u32[]{:S(2)}) async-start(bf16[16,8,8192]{2,1,0:T(8,128)(2,1)} %fusion.4), calls=%async_computation.1 | async-start | bytes 4194304 | tf_op jit(solution)/shard_map/all_to_all | solution.py:77
  148.6 25.2 %collective-permute-done.5 = bf16[32,8192]{1,0:T(8,128)(2,1)S(1)} collective-permute-done((bf16[32,8192]{1,0:T(8,128)(2,1)S(1)}, bf16[32,8192]{1,0:T(8,128)(2,1)S(1)}, u32[]{:S(2)}, u32[]{:S(2)}) %collective-permute-start.5) | collective-permute-done | bytes 524320 | tf_op jit(solution)/shard_map/ppermute | solution.py:19
  174.8 19.9 %all-to-all-done.1 = bf16[16,8,8192]{2,1,0:T(8,128)(2,1)} async-done(((bf16[16,8,8192]{2,1,0:T(8,128)(2,1)}), bf16[16,8,8192]{2,1,0:T(8,128)(2,1)}, u32[]{:S(2)}, u32[]{:S(2)}) %all-to-all-start.1) | async-done | bytes 2097184 | tf_op jit(solution)/shard_map/all_to_all | solution.py:77
  205.9 2.4 fusion.11
  208.3 2.1 fusion.5
  210.4 4.9 %all-to-all-start.3 = ((bf16[16,8,8192]{2,1,0:T(8,128)(2,1)}), bf16[16,8,8192]{2,1,0:T(8,128)(2,1)}, u32[]{:S(2)}, u32[]{:S(2)}) async-start(bf16[16,8,8192]{2,1,0:T(8,128)(2,1)} %fusion.5), calls=%async_computation.3 | async-start | bytes 4194304 | tf_op jit(solution)/shard_map/all_to_all | solution.py:77
  217.3 24.6 %collective-permute-done.8 = bf16[32,8192]{1,0:T(8,128)(2,1)S(1)} collective-permute-done((bf16[32,8192]{1,0:T(8,128)(2,1)S(1)}, bf16[32,8192]{1,0:T(8,128)(2,1)S(1)}, u32[]{:S(2)}, u32[]{:S(2)}) %collective-permute-start.8) | collective-permute-done | bytes 524320 | tf_op jit(solution)/shard_map/ppermute | solution.py:19
  245.1 18.1 %all-to-all-done.3 = bf16[16,8,8192]{2,1,0:T(8,128)(2,1)} async-done(((bf16[16,8,8192]{2,1,0:T(8,128)(2,1)}), bf16[16,8,8192]{2,1,0:T(8,128)(2,1)}, u32[]{:S(2)}, u32[]{:S(2)}) %all-to-all-start.3) | async-done | bytes 2097184 | tf_op jit(solution)/shard_map/all_to_all | solution.py:77
  266.9 1.9 collective-permute-start.10
  268.8 13.6 %collective-permute-done.10 = bf16[32,8192]{1,0:T(8,128)(2,1)S(1)} collective-permute-done((bf16[32,8192]{1,0:T(8,128)(2,1)S(1)}, bf16[32,8192]{1,0:T(8,128)(2,1)S(1)}, u32[]{:S(2)}, u32[]{:S(2)}) %collective-permute-start.10) | collective-permute-done | bytes 524320 | tf_op jit(solution)/shard_map/ppermute | solution.py:50
  282.4 2.1 add_convert_fusion
  284.6 2.1 collective-permute-start.11
  286.6 4.3 %fusion.25 = f32[128,8192]{1,0:T(8,128)} fusion(pred[152,128]{1,0:T(8,128)(4,1)S(1)} %iota_compare_fusion, bf16[16,8,8192]{2,1,0:T(8,128)(2,1)} %all-to-all-done.1), kind=kOutput, calls=%fused_computation.70 | convolution fusion | flops 268435456 | bytes 6307840 | tf_op jit(solution)/shard_map/dot_general | solution.py:15
  290.9 3.1 fusion
  298.5 4.3 %fusion.22 = f32[128,8192]{1,0:T(8,128)} fusion(pred[152,128]{1,0:T(8,128)(4,1)S(1)} %iota_compare_fusion, bf16[16,8,8192]{2,1,0:T(8,128)(2,1)} %all-to-all-done.3), kind=kOutput, calls=%fused_computation.67 | convolution fusion | flops 268435456 | bytes 6307840 | tf_op jit(solution)/shard_map/dot_general | solution.py:15
  302.8 4.7 %fusion.1 = bf16[128,8192]{1,0:T(8,128)(2,1)} fusion(f32[128,8192]{1,0:T(8,128)} %fusion.22, bf16[24,64]{1,0:T(8,128)(2,1)S(1)} %fusion.13, bf16[64,8192]{1,0:T(8,128)(2,1)S(1)} %maximum_add_fusion, bf16[64,8192]{1,0:T(8,128)(2,1)} %collective-permute-done.6, pred[]{:T(512)S(6)} %eq.70, pred[152,128]{1,0:T(8,128)(4,1)S(1)} %iota_compare_fusion), kind=kOutput, calls=%fused_computation.3 | convolution fusion | flops 78315520 | bytes 8397825 | tf_op jit(solution)/shard_map/dot_general | solution.py:15
  310.9 2.2 collective-permute-start.13
  313.1 2.0 convolution_convert_fusion.5
  315.2 2.0 convolution_convert_fusion.4
  (86 shorter events, 41.3 us)
Async XLA Ops:
  0.6 18.7 %copy-start = (bf16[128,8192]{1,0:T(8,128)(2,1)S(1)}, bf16[128,8192]{1,0:T(8,128)(2,1)}, u32[]{:S(2)}) copy-start(bf16[128,8192]{1,0:T(8,128)(2,1)} %param.7) | copy-start | bytes 6291460
  4.9 1.3 copy-start.10
  6.2 0.8 copy-start.14
  6.2 1.7 copy-start.8
  6.3 10.1 %collective-permute-start = (bf16[64,8192]{1,0:T(8,128)(2,1)S(1)}, bf16[64,8192]{1,0:T(8,128)(2,1)}, u32[]{:S(2)}, u32[]{:S(2)}) collective-permute-start(bf16[64,8192]{1,0:T(8,128)(2,1)S(1)} %constant_dynamic-slice_fusion.1), channel_id=1, source_target_pairs={{0,1},{1,0},{2,3},{3,2},{4,5},{5,4},{6,7},{7,6},{8,9},{9,8},{10,11... | collective-permute-start | bytes 3145736 | tf_op jit(solution)/shard_map/ppermute | solution.py:19
  10.0 54.0 %all-to-all-start = ((bf16[16,8,8192]{2,1,0:T(8,128)(2,1)}), bf16[16,8,8192]{2,1,0:T(8,128)(2,1)}, u32[]{:S(2)}, u32[]{:S(2)}) async-start(bf16[16,8,8192]{2,1,0:T(8,128)(2,1)} %fusion.2), calls=%async_computation | async-start | bytes 4194304 | tf_op jit(solution)/shard_map/all_to_all | solution.py:77
  19.0 49.9 %collective-permute-start.1 = (bf16[32,8192]{1,0:T(8,128)(2,1)}, bf16[32,8192]{1,0:T(8,128)(2,1)}, u32[]{:S(2)}, u32[]{:S(2)}) collective-permute-start(bf16[32,8192]{1,0:T(8,128)(2,1)} %constant_dynamic-slice_fusion), channel_id=1, source_target_pairs={{0,2},{1,3},{2,0},{3,1},{4,6},{5,7},{6,4},{7,5},{8,10},{9,11},{10,... | collective-permute-start | bytes 1572872 | tf_op jit(solution)/shard_map/ppermute | solution.py:19
  64.0 70.0 %all-to-all-start.2 = ((bf16[16,8,8192]{2,1,0:T(8,128)(2,1)}), bf16[16,8,8192]{2,1,0:T(8,128)(2,1)}, u32[]{:S(2)}, u32[]{:S(2)}) async-start(bf16[16,8,8192]{2,1,0:T(8,128)(2,1)} %fusion.3), calls=%async_computation.2 | async-start | bytes 4194304 | tf_op jit(solution)/shard_map/all_to_all | solution.py:77
  70.1 45.6 %collective-permute-start.2 = (bf16[32,8192]{1,0:T(8,128)(2,1)S(1)}, bf16[32,8192]{1,0:T(8,128)(2,1)S(1)}, u32[]{:S(2)}, u32[]{:S(2)}) collective-permute-start(bf16[32,8192]{1,0:T(8,128)(2,1)S(1)} %dynamic-slice_add_fusion.1), channel_id=1, source_target_pairs={{0,4},{1,5},{2,6},{3,7},{12,8},{13,9},{14,10},{15,11},{16,20},{17,... | collective-permute-start | bytes 1572872 | tf_op jit(solution)/shard_map/ppermute | solution.py:50
  115.8 22.8 %copy-start.5 = (bf16[1,64,8192]{2,1,0:T(8,128)(2,1)S(1)}, bf16[1,64,8192]{2,1,0:T(8,128)(2,1)}, u32[]{:S(2)}) copy-start(bf16[1,64,8192]{2,1,0:T(8,128)(2,1)} %param.9) | copy-start | bytes 3145732
  115.8 15.2 %collective-permute-start.3 = (bf16[32,8192]{1,0:T(8,128)(2,1)S(1)}, bf16[32,8192]{1,0:T(8,128)(2,1)S(1)}, u32[]{:S(2)}, u32[]{:S(2)}) collective-permute-start(bf16[32,8192]{1,0:T(8,128)(2,1)S(1)} %add_add_fusion.1), channel_id=1, source_target_pairs={{4,8},{5,9},{6,10},{7,11},{8,4},{9,5},{10,6},{11,7},{20,24},{21,25... | collective-permute-start | bytes 1572872 | tf_op jit(solution)/shard_map/ppermute | solution.py:50
  131.9 15.2 %collective-permute-start.4 = (bf16[32,8192]{1,0:T(8,128)(2,1)}, bf16[32,8192]{1,0:T(8,128)(2,1)}, u32[]{:S(2)}, u32[]{:S(2)}) collective-permute-start(bf16[32,8192]{1,0:T(8,128)(2,1)} %add.136), channel_id=1, source_target_pairs={{4,0},{5,1},{6,2},{7,3},{8,12},{9,13},{10,14},{11,15},{20,16},{21,... | collective-permute-start | bytes 1572872 | tf_op jit(solution)/shard_map/ppermute | solution.py:50
  140.7 54.1 %all-to-all-start.1 = ((bf16[16,8,8192]{2,1,0:T(8,128)(2,1)}), bf16[16,8,8192]{2,1,0:T(8,128)(2,1)}, u32[]{:S(2)}, u32[]{:S(2)}) async-start(bf16[16,8,8192]{2,1,0:T(8,128)(2,1)} %fusion.4), calls=%async_computation.1 | async-start | bytes 4194304 | tf_op jit(solution)/shard_map/all_to_all | solution.py:77
  148.3 25.5 %collective-permute-start.5 = (bf16[32,8192]{1,0:T(8,128)(2,1)S(1)}, bf16[32,8192]{1,0:T(8,128)(2,1)S(1)}, u32[]{:S(2)}, u32[]{:S(2)}) collective-permute-start(bf16[32,8192]{1,0:T(8,128)(2,1)S(1)} %select_add_fusion), channel_id=1, source_target_pairs={{0,2},{1,3},{2,0},{3,1},{4,6},{5,7},{6,4},{7,5},{8,10},{9,11},{10,... | collective-permute-start | bytes 1572872 | tf_op jit(solution)/shard_map/ppermute | solution.py:19
  198.0 2.9 collective-permute-start.6
  198.3 1.6 copy-start.9
  203.9 1.7 copy-start.2
  203.9 2.0 copy-start.6
  205.5 2.8 copy-start.7
  205.5 9.8 %collective-permute-start.7 = (bf16[64,8192]{1,0:T(8,128)(2,1)}, bf16[64,8192]{1,0:T(8,128)(2,1)}, u32[]{:S(2)}, u32[]{:S(2)}) collective-permute-start(bf16[64,8192]{1,0:T(8,128)(2,1)} %fusion.7), channel_id=1, source_target_pairs={{0,1},{1,0},{2,3},{3,2},{4,5},{5,4},{6,7},{7,6},{8,9},{9,8},{10,11... | collective-permute-start | bytes 3145736 | tf_op jit(solution)/shard_map/ppermute | solution.py:19
  210.4 52.8 %all-to-all-start.3 = ((bf16[16,8,8192]{2,1,0:T(8,128)(2,1)}), bf16[16,8,8192]{2,1,0:T(8,128)(2,1)}, u32[]{:S(2)}, u32[]{:S(2)}) async-start(bf16[16,8,8192]{2,1,0:T(8,128)(2,1)} %fusion.5), calls=%async_computation.3 | async-start | bytes 4194304 | tf_op jit(solution)/shard_map/all_to_all | solution.py:77
  216.9 25.0 %copy-start.3 = (f32[64,8192]{1,0:T(8,128)}, f32[64,8192]{1,0:T(8,128)S(1)}, u32[]{:S(2)}) copy-start(f32[64,8192]{1,0:T(8,128)S(1)} %fusion.9) | copy-start | bytes 6291460
  217.0 25.0 %collective-permute-start.8 = (bf16[32,8192]{1,0:T(8,128)(2,1)S(1)}, bf16[32,8192]{1,0:T(8,128)(2,1)S(1)}, u32[]{:S(2)}, u32[]{:S(2)}) collective-permute-start(bf16[32,8192]{1,0:T(8,128)(2,1)S(1)} %dynamic-slice_convert_fusion), channel_id=1, source_target_pairs={{0,2},{1,3},{2,0},{3,1},{4,6},{5,7},{6,4},{7,5},{8,10},{9,11},{10,... | collective-permute-start | bytes 1572872 | tf_op jit(solution)/shard_map/ppermute | solution.py:19
  243.7 38.8 %copy-start.4 = (f32[64,8192]{1,0:T(8,128)S(1)}, f32[64,8192]{1,0:T(8,128)}, u32[]{:S(2)}) copy-start(f32[64,8192]{1,0:T(8,128)} %copy-done.3) | copy-start | bytes 6291460
  243.7 21.5 %collective-permute-start.9 = (bf16[32,8192]{1,0:T(8,128)(2,1)}, bf16[32,8192]{1,0:T(8,128)(2,1)}, u32[]{:S(2)}, u32[]{:S(2)}) collective-permute-start(bf16[32,8192]{1,0:T(8,128)(2,1)} %fusion.18), channel_id=1, source_target_pairs={{0,4},{1,5},{2,6},{3,7},{12,8},{13,9},{14,10},{15,11},{16,20},{17,... | collective-permute-start | bytes 1572872 | tf_op jit(solution)/shard_map/ppermute | solution.py:50
  263.2 19.2 %copy-start.12 = (bf16[32,8192]{1,0:T(8,128)(2,1)S(1)}, bf16[32,8192]{1,0:T(8,128)(2,1)}, u32[]{:S(2)}) copy-start(bf16[32,8192]{1,0:T(8,128)(2,1)} %copy-done.11) | copy-start | bytes 1572868
  266.9 15.5 %collective-permute-start.10 = (bf16[32,8192]{1,0:T(8,128)(2,1)S(1)}, bf16[32,8192]{1,0:T(8,128)(2,1)S(1)}, u32[]{:S(2)}, u32[]{:S(2)}) collective-permute-start(bf16[32,8192]{1,0:T(8,128)(2,1)S(1)} %fusion.15), channel_id=1, source_target_pairs={{4,8},{5,9},{6,10},{7,11},{8,4},{9,5},{10,6},{11,7},{20,24},{21,25... | collective-permute-start | bytes 1572872 | tf_op jit(solution)/shard_map/ppermute | solution.py:50
  284.6 12.5 %collective-permute-start.11 = (bf16[32,8192]{1,0:T(8,128)(2,1)}, bf16[32,8192]{1,0:T(8,128)(2,1)}, u32[]{:S(2)}, u32[]{:S(2)}) collective-permute-start(bf16[32,8192]{1,0:T(8,128)(2,1)} %add_convert_fusion), channel_id=1, source_target_pairs={{4,0},{5,1},{6,2},{7,3},{8,12},{9,13},{10,14},{11,15},{20,16},{21,... | collective-permute-start | bytes 1572872 | tf_op jit(solution)/shard_map/ppermute | solution.py:50
  294.0 3.0 copy-start.13
  298.4 12.2 %collective-permute-start.12 = (bf16[32,8192]{1,0:T(8,128)(2,1)S(1)}, bf16[32,8192]{1,0:T(8,128)(2,1)S(1)}, u32[]{:S(2)}, u32[]{:S(2)}) collective-permute-start(bf16[32,8192]{1,0:T(8,128)(2,1)S(1)} %fusion.16), channel_id=1, source_target_pairs={{0,2},{1,3},{2,0},{3,1},{4,6},{5,7},{6,4},{7,5},{8,10},{9,11},{10,... | collective-permute-start | bytes 1572872 | tf_op jit(solution)/shard_map/ppermute | solution.py:19
  310.9 6.3 %collective-permute-start.13 = (bf16[64,8192]{1,0:T(8,128)(2,1)S(1)}, bf16[64,8192]{1,0:T(8,128)(2,1)S(1)}, u32[]{:S(2)}, u32[]{:S(2)}) collective-permute-start(bf16[64,8192]{1,0:T(8,128)(2,1)S(1)} %maximum_add_fusion.1), channel_id=1, source_target_pairs={{0,1},{1,0},{2,3},{3,2},{4,5},{5,4},{6,7},{7,6},{8,9},{9,8},{10,11... | collective-permute-start | bytes 3145736 | tf_op jit(solution)/shard_map/ppermute | solution.py:19
  317.4 2.0 copy-start.1
  (1 other events, 0.8 us)

commit v3 on v2

--- a/solution.py
+++ b/solution.py
@@ -64,12 +64,12 @@
 def sum_over_owner(x, me, owners, wire, ties):
     if owners & (owners - 1) or owners < 8:
         return lax.psum(x, "owner").astype(BF)
-    middle, third, last = ties
+    middle, third, last, final = ties
     x = halve(x, 0, me, owners, wire)
     x = halve(x, 1, me, owners, wire)
     x = line_sum(x, me, owners, 4, wire, middle).astype(BF)
-    x = double(after(x, third), 1, me, owners)
-    return double(after(x, last), 0, me, owners)
+    x = double(after(after(x, third), last), 1, me, owners)
+    return double(after(x, final), 0, me, owners)
 
 
 def exchange(x, owners):
@@ -116,11 +116,11 @@
     activated, hid_grad = gate(rows_by_rows(got_rows, down_mat), rows_by_rows(got_cot, up_mat))
     back_out = exchange(pick(activated, up_mat), owners)
     back_grad = exchange(pick(hid_grad, down_mat), owners)
-    own_sums = jnp.concatenate([outer_sum(hid_grad, got_rows), outer_sum(activated, got_cot)], 0)
+    own_sums = jnp.concatenate([outer_sum(hid_grad, got_rows), outer_sum(activated, got_cot)], 0).astype(BF)
 
     both = jnp.concatenate([down_mat, up_mat], 0)
     both = jnp.where(me == busy, both, jnp.zeros_like(both))
-    both = sum_over_owner(both, me, owners, BF, (got_rows, got_cot, back_out))
+    both = sum_over_owner(both, me, owners, BF, (got_rows, got_cot, got_cot, back_out))
     busy_down, busy_up = both[:rank], both[rank:]
     busy_rows = pick(place_busy, tokens)
     busy_cot = pick(place_busy, cotangent)
@@ -133,8 +133,8 @@
 
     adapter_out = put(back_out, pick(busy_act, busy_up))
     input_grad = put(back_grad, pick(busy_hid, busy_down))
-    busy_sums = sum_over_owner(busy_sums, me, owners, BF, (back_grad, adapter_out, input_grad))
-    sums = jnp.where(me == busy, busy_sums, own_sums.astype(BF))
+    busy_sums = sum_over_owner(busy_sums, me, owners, BF, (back_grad, input_grad, adapter_out, own_sums))
+    sums = jnp.where(me == busy, busy_sums, own_sums)
     return adapter_out, input_grad, sums[:rank][None], sums[rank:][None]
 
 

time: 323 us -> 320 us (level)
    ppermute x6, waiting for transfers between devices: 69.3 us -> 58.2 us  [hop(): return lax.ppermute(y.astype(wire), 'owner', pairs).astype(x.dtype)]
    ppermute x8, waiting for transfers between devices: 51.7 us -> 59.8 us  [flip(): return lax.ppermute(x, 'owner', [(i, i ^ 1 << bit) for i in range(owners)])]
    slice x6 -> x7, local copies, waits for them, and re-layouts: 6.56 us -> 7 us  [after(): other[0, 0].astype(F32)]
where the time goes in v3:
time: 320 us; the launch traced here: 316 us
  waiting for transfers between devices  200 us (62%)
  starting transfers between devices  39.6 us (12%)
  matrix products  37.9 us (12%)
  other arithmetic  19.7 us (6%)
  local copies, waits for them, and re-layouts  12.6 us (4%)
  between operations  6.36 us (2%)
    all_to_all x4, waiting for transfers between devices, exchange(): y = lax.all_to_all(y, 'owner', split_axis=0, concat_axis=0, tiled=True)  82.2 us
    ppermute x8, waiting for transfers between devices, flip(): return lax.ppermute(x, 'owner', [(i, i ^ 1 << bit) for i in range(owners)])  59.8 us
    ppermute x6, waiting for transfers between devices, hop(): return lax.ppermute(y.astype(wire), 'owner', pairs).astype(x.dtype)  58.2 us
    all_to_all x4, starting transfers between devices, exchange(): y = lax.all_to_all(y, 'owner', split_axis=0, concat_axis=0, tiled=True)  22.7 us
    dot_general x8, matrix products, outer_sum(): lax.dot_general(a, b, (((0,), (0,)), ((), ())), preferred_element_type=F32)  21.6 us
    ppermute x6, starting transfers between devices, hop(): return lax.ppermute(y.astype(wire), 'owner', pairs).astype(x.dtype)  12.7 us
    dot_general x6, matrix products, pick(): return jnp.dot(which, rows, preferred_element_type=F32).astype(BF)  8.93 us
    dot_general x4, matrix products, rows_by_rows(): lax.dot_general(a, b, (((1,), (1,)), ((), ())), preferred_element_type=F32)  7.19 us
  transfers between devices with their start and end apart: 18, of which 11 were waited for; matrix products, arithmetic and copies ran while one was open for 16% of the time, Pallas kernels for 0%

profile of v3, /device:TPU:11, one launch (start us, length us, event | category | flops | bytes accessed | tf_op | source)
XLA Modules:
  0.0 316.4 jit_solution(12421306031158726848)
XLA Ops:
  2.9 2.0 maximum_select_fusion
  8.0 2.0 fusion.2
  10.0 6.4 %all-to-all-start = ((bf16[16,8,8192]{2,1,0:T(8,128)(2,1)}), bf16[16,8,8192]{2,1,0:T(8,128)(2,1)}, u32[]{:S(2)}, u32[]{:S(2)}) async-start(bf16[16,8,8192]{2,1,0:T(8,128)(2,1)} %fusion.2), calls=%async_computation | async-start | bytes 4194304 | tf_op jit(solution)/shard_map/all_to_all | solution.py:77
  16.4 1.8 dynamic-slice_add_fusion
  19.3 2.0 fusion.3
  21.3 42.7 %all-to-all-done = bf16[16,8,8192]{2,1,0:T(8,128)(2,1)} async-done(((bf16[16,8,8192]{2,1,0:T(8,128)(2,1)}), bf16[16,8,8192]{2,1,0:T(8,128)(2,1)}, u32[]{:S(2)}, u32[]{:S(2)}) %all-to-all-start) | async-done | bytes 2097184 | tf_op jit(solution)/shard_map/all_to_all | solution.py:77
  64.0 4.9 %all-to-all-start.2 = ((bf16[16,8,8192]{2,1,0:T(8,128)(2,1)}), bf16[16,8,8192]{2,1,0:T(8,128)(2,1)}, u32[]{:S(2)}, u32[]{:S(2)}) async-start(bf16[16,8,8192]{2,1,0:T(8,128)(2,1)} %fusion.3), calls=%async_computation.2 | async-start | bytes 4194304 | tf_op jit(solution)/shard_map/all_to_all | solution.py:77
  73.3 42.5 %collective-permute-done.2 = bf16[32,8192]{1,0:T(8,128)(2,1)S(1)} collective-permute-done((bf16[32,8192]{1,0:T(8,128)(2,1)S(1)}, bf16[32,8192]{1,0:T(8,128)(2,1)S(1)}, u32[]{:S(2)}, u32[]{:S(2)}) %collective-permute-start.2) | collective-permute-done | bytes 524320 | tf_op jit(solution)/shard_map/ppermute | solution.py:50
  115.8 3.8 %collective-permute-start.3 = (bf16[32,8192]{1,0:T(8,128)(2,1)S(1)}, bf16[32,8192]{1,0:T(8,128)(2,1)S(1)}, u32[]{:S(2)}, u32[]{:S(2)}) collective-permute-start(bf16[32,8192]{1,0:T(8,128)(2,1)S(1)} %add_add_fusion.2), channel_id=1, source_target_pairs={{4,8},{5,9},{6,10},{7,11},{8,4},{9,5},{10,6},{11,7},{20,24},{21,25... | collective-permute-start | bytes 1572872 | tf_op jit(solution)/shard_map/ppermute | solution.py:50
  119.6 11.4 %collective-permute-done.3 = bf16[32,8192]{1,0:T(8,128)(2,1)S(1)} collective-permute-done((bf16[32,8192]{1,0:T(8,128)(2,1)S(1)}, bf16[32,8192]{1,0:T(8,128)(2,1)S(1)}, u32[]{:S(2)}, u32[]{:S(2)}) %collective-permute-start.3) | collective-permute-done | bytes 524320 | tf_op jit(solution)/shard_map/ppermute | solution.py:50
  131.9 2.1 collective-permute-start.4
  135.9 2.7 fusion.44
  138.6 2.1 fusion.4
  140.7 6.5 %all-to-all-start.1 = ((bf16[16,8,8192]{2,1,0:T(8,128)(2,1)}), bf16[16,8,8192]{2,1,0:T(8,128)(2,1)}, u32[]{:S(2)}, u32[]{:S(2)}) async-start(bf16[16,8,8192]{2,1,0:T(8,128)(2,1)} %fusion.4), calls=%async_computation.1 | async-start | bytes 4194304 | tf_op jit(solution)/shard_map/all_to_all | solution.py:77
  148.6 25.2 %collective-permute-done.5 = bf16[32,8192]{1,0:T(8,128)(2,1)S(1)} collective-permute-done((bf16[32,8192]{1,0:T(8,128)(2,1)S(1)}, bf16[32,8192]{1,0:T(8,128)(2,1)S(1)}, u32[]{:S(2)}, u32[]{:S(2)}) %collective-permute-start.5) | collective-permute-done | bytes 524320 | tf_op jit(solution)/shard_map/ppermute | solution.py:19
  174.8 19.9 %all-to-all-done.1 = bf16[16,8,8192]{2,1,0:T(8,128)(2,1)} async-done(((bf16[16,8,8192]{2,1,0:T(8,128)(2,1)}), bf16[16,8,8192]{2,1,0:T(8,128)(2,1)}, u32[]{:S(2)}, u32[]{:S(2)}) %all-to-all-start.1) | async-done | bytes 2097184 | tf_op jit(solution)/shard_map/all_to_all | solution.py:77
  205.9 2.4 fusion.11
  208.3 2.1 fusion.5
  210.4 4.9 %all-to-all-start.3 = ((bf16[16,8,8192]{2,1,0:T(8,128)(2,1)}), bf16[16,8,8192]{2,1,0:T(8,128)(2,1)}, u32[]{:S(2)}, u32[]{:S(2)}) async-start(bf16[16,8,8192]{2,1,0:T(8,128)(2,1)} %fusion.5), calls=%async_computation.3 | async-start | bytes 4194304 | tf_op jit(solution)/shard_map/all_to_all | solution.py:77
  217.3 24.6 %collective-permute-done.8 = bf16[32,8192]{1,0:T(8,128)(2,1)S(1)} collective-permute-done((bf16[32,8192]{1,0:T(8,128)(2,1)S(1)}, bf16[32,8192]{1,0:T(8,128)(2,1)S(1)}, u32[]{:S(2)}, u32[]{:S(2)}) %collective-permute-start.8) | collective-permute-done | bytes 524320 | tf_op jit(solution)/shard_map/ppermute | solution.py:19
  243.4 19.5 %all-to-all-done.3 = bf16[16,8,8192]{2,1,0:T(8,128)(2,1)} async-done(((bf16[16,8,8192]{2,1,0:T(8,128)(2,1)}), bf16[16,8,8192]{2,1,0:T(8,128)(2,1)}, u32[]{:S(2)}, u32[]{:S(2)}) %all-to-all-start.3) | async-done | bytes 2097184 | tf_op jit(solution)/shard_map/all_to_all | solution.py:77
  266.4 2.1 collective-permute-start.10
  268.5 4.3 %fusion.23 = f32[128,8192]{1,0:T(8,128)} fusion(pred[152,128]{1,0:T(8,128)(4,1)S(1)} %iota_compare_fusion, bf16[16,8,8192]{2,1,0:T(8,128)(2,1)} %all-to-all-done.3), kind=kOutput, calls=%fused_computation.68 | convolution fusion | flops 268435456 | bytes 6307840 | tf_op jit(solution)/shard_map/dot_general | solution.py:15
  272.8 4.4 %fusion.26 = f32[128,8192]{1,0:T(8,128)} fusion(pred[152,128]{1,0:T(8,128)(4,1)S(1)} %iota_compare_fusion, bf16[16,8,8192]{2,1,0:T(8,128)(2,1)} %all-to-all-done.1), kind=kOutput, calls=%fused_computation.71 | convolution fusion | flops 268435456 | bytes 6307840 | tf_op jit(solution)/shard_map/dot_general | solution.py:15
  277.3 4.3 %collective-permute-done.10 = bf16[32,8192]{1,0:T(8,128)(2,1)S(1)} collective-permute-done((bf16[32,8192]{1,0:T(8,128)(2,1)S(1)}, bf16[32,8192]{1,0:T(8,128)(2,1)S(1)}, u32[]{:S(2)}, u32[]{:S(2)}) %collective-permute-start.10) | collective-permute-done | bytes 524320 | tf_op jit(solution)/shard_map/ppermute | solution.py:50
  282.7 2.1 collective-permute-start.11
  284.8 3.4 %fusion.1 = bf16[128,8192]{1,0:T(8,128)(2,1)S(1)} fusion(f32[128,8192]{1,0:T(8,128)} %fusion.23, bf16[24,64]{1,0:T(8,128)(2,1)S(1)} %fusion.13, bf16[64,8192]{1,0:T(8,128)(2,1)S(1)} %maximum_add_fusion, bf16[64,8192]{1,0:T(8,128)(2,1)} %collective-permute-done.6, pred[]{:T(512)S(6)} %eq.70, pred[152,128]{1,0:T(8,128)(4,1)S(1)} %iota_compare_fusion), kind=kOutput, calls=%fused_computation.3 | convolution fusion | flops 78315520 | bytes 8397825 | tf_op jit(solution)/shard_map/dot_general | solution.py:15
  289.5 4.4 %fusion = bf16[128,8192]{1,0:T(8,128)(2,1)} fusion(f32[128,8192]{1,0:T(8,128)} %fusion.26, bf16[64,8192]{1,0:T(8,128)(2,1)} %collective-permute-done.6, bf16[64,8192]{1,0:T(8,128)(2,1)S(1)} %maximum_add_fusion, pred[]{:T(512)S(6)} %eq.70, pred[152,128]{1,0:T(8,128)(4,1)S(1)} %iota_compare_fusion, f32[24,64]{1,0:T(8,128)S(1)} %fusion.18), kind=kOutput, calls=%fused_computation.2 | convolution fusion | flops 78323200 | bytes 8403969 | tf_op jit(solution)/shard_map/dot_general | solution.py:15
  297.2 2.0 convolution_convert_fusion.5
  300.5 9.2 %collective-permute-done.12 = bf16[32,8192]{1,0:T(8,128)(2,1)S(1)} collective-permute-done((bf16[32,8192]{1,0:T(8,128)(2,1)S(1)}, bf16[32,8192]{1,0:T(8,128)(2,1)S(1)}, u32[]{:S(2)}, u32[]{:S(2)}) %collective-permute-start.12) | collective-permute-done | bytes 524320 | tf_op jit(solution)/shard_map/ppermute | solution.py:19
  309.9 2.0 collective-permute-start.13
  311.9 2.0 convolution_convert_fusion.4
  (91 shorter events, 38.2 us)
Async XLA Ops:
  0.6 18.7 %copy-start = (bf16[128,8192]{1,0:T(8,128)(2,1)S(1)}, bf16[128,8192]{1,0:T(8,128)(2,1)}, u32[]{:S(2)}) copy-start(bf16[128,8192]{1,0:T(8,128)(2,1)} %param.7) | copy-start | bytes 6291460
  6.2 1.7 copy-start.8
  6.3 10.1 %collective-permute-start = (bf16[64,8192]{1,0:T(8,128)(2,1)S(1)}, bf16[64,8192]{1,0:T(8,128)(2,1)}, u32[]{:S(2)}, u32[]{:S(2)}) collective-permute-start(bf16[64,8192]{1,0:T(8,128)(2,1)S(1)} %constant_dynamic-slice_fusion.1), channel_id=1, source_target_pairs={{0,1},{1,0},{2,3},{3,2},{4,5},{5,4},{6,7},{7,6},{8,9},{9,8},{10,11... | collective-permute-start | bytes 3145736 | tf_op jit(solution)/shard_map/ppermute | solution.py:19
  10.0 54.0 %all-to-all-start = ((bf16[16,8,8192]{2,1,0:T(8,128)(2,1)}), bf16[16,8,8192]{2,1,0:T(8,128)(2,1)}, u32[]{:S(2)}, u32[]{:S(2)}) async-start(bf16[16,8,8192]{2,1,0:T(8,128)(2,1)} %fusion.2), calls=%async_computation | async-start | bytes 4194304 | tf_op jit(solution)/shard_map/all_to_all | solution.py:77
  19.0 49.9 %collective-permute-start.1 = (bf16[32,8192]{1,0:T(8,128)(2,1)}, bf16[32,8192]{1,0:T(8,128)(2,1)}, u32[]{:S(2)}, u32[]{:S(2)}) collective-permute-start(bf16[32,8192]{1,0:T(8,128)(2,1)} %constant_dynamic-slice_fusion), channel_id=1, source_target_pairs={{0,2},{1,3},{2,0},{3,1},{4,6},{5,7},{6,4},{7,5},{8,10},{9,11},{10,... | collective-permute-start | bytes 1572872 | tf_op jit(solution)/shard_map/ppermute | solution.py:19
  64.0 70.0 %all-to-all-start.2 = ((bf16[16,8,8192]{2,1,0:T(8,128)(2,1)}), bf16[16,8,8192]{2,1,0:T(8,128)(2,1)}, u32[]{:S(2)}, u32[]{:S(2)}) async-start(bf16[16,8,8192]{2,1,0:T(8,128)(2,1)} %fusion.3), calls=%async_computation.2 | async-start | bytes 4194304 | tf_op jit(solution)/shard_map/all_to_all | solution.py:77
  70.1 45.6 %collective-permute-start.2 = (bf16[32,8192]{1,0:T(8,128)(2,1)S(1)}, bf16[32,8192]{1,0:T(8,128)(2,1)S(1)}, u32[]{:S(2)}, u32[]{:S(2)}) collective-permute-start(bf16[32,8192]{1,0:T(8,128)(2,1)S(1)} %dynamic-slice_add_fusion.1), channel_id=1, source_target_pairs={{0,4},{1,5},{2,6},{3,7},{12,8},{13,9},{14,10},{15,11},{16,20},{17,... | collective-permute-start | bytes 1572872 | tf_op jit(solution)/shard_map/ppermute | solution.py:50
  115.8 22.8 %copy-start.5 = (bf16[1,64,8192]{2,1,0:T(8,128)(2,1)S(1)}, bf16[1,64,8192]{2,1,0:T(8,128)(2,1)}, u32[]{:S(2)}) copy-start(bf16[1,64,8192]{2,1,0:T(8,128)(2,1)} %param.9) | copy-start | bytes 3145732
  115.8 15.2 %collective-permute-start.3 = (bf16[32,8192]{1,0:T(8,128)(2,1)S(1)}, bf16[32,8192]{1,0:T(8,128)(2,1)S(1)}, u32[]{:S(2)}, u32[]{:S(2)}) collective-permute-start(bf16[32,8192]{1,0:T(8,128)(2,1)S(1)} %add_add_fusion.2), channel_id=1, source_target_pairs={{4,8},{5,9},{6,10},{7,11},{8,4},{9,5},{10,6},{11,7},{20,24},{21,25... | collective-permute-start | bytes 1572872 | tf_op jit(solution)/shard_map/ppermute | solution.py:50
  131.9 15.2 %collective-permute-start.4 = (bf16[32,8192]{1,0:T(8,128)(2,1)}, bf16[32,8192]{1,0:T(8,128)(2,1)}, u32[]{:S(2)}, u32[]{:S(2)}) collective-permute-start(bf16[32,8192]{1,0:T(8,128)(2,1)} %add.146), channel_id=1, source_target_pairs={{4,0},{5,1},{6,2},{7,3},{8,12},{9,13},{10,14},{11,15},{20,16},{21,... | collective-permute-start | bytes 1572872 | tf_op jit(solution)/shard_map/ppermute | solution.py:50
  140.7 54.1 %all-to-all-start.1 = ((bf16[16,8,8192]{2,1,0:T(8,128)(2,1)}), bf16[16,8,8192]{2,1,0:T(8,128)(2,1)}, u32[]{:S(2)}, u32[]{:S(2)}) async-start(bf16[16,8,8192]{2,1,0:T(8,128)(2,1)} %fusion.4), calls=%async_computation.1 | async-start | bytes 4194304 | tf_op jit(solution)/shard_map/all_to_all | solution.py:77
  148.3 25.5 %collective-permute-start.5 = (bf16[32,8192]{1,0:T(8,128)(2,1)S(1)}, bf16[32,8192]{1,0:T(8,128)(2,1)S(1)}, u32[]{:S(2)}, u32[]{:S(2)}) collective-permute-start(bf16[32,8192]{1,0:T(8,128)(2,1)S(1)} %add_add_fusion.1), channel_id=1, source_target_pairs={{0,2},{1,3},{2,0},{3,1},{4,6},{5,7},{6,4},{7,5},{8,10},{9,11},{10,... | collective-permute-start | bytes 1572872 | tf_op jit(solution)/shard_map/ppermute | solution.py:19
  198.0 2.9 collective-permute-start.6
  203.9 1.7 copy-start.2
  203.9 2.0 copy-start.6
  205.5 2.8 copy-start.7
  205.5 9.8 %collective-permute-start.7 = (bf16[64,8192]{1,0:T(8,128)(2,1)}, bf16[64,8192]{1,0:T(8,128)(2,1)}, u32[]{:S(2)}, u32[]{:S(2)}) collective-permute-start(bf16[64,8192]{1,0:T(8,128)(2,1)} %fusion.7), channel_id=1, source_target_pairs={{0,1},{1,0},{2,3},{3,2},{4,5},{5,4},{6,7},{7,6},{8,9},{9,8},{10,11... | collective-permute-start | bytes 3145736 | tf_op jit(solution)/shard_map/ppermute | solution.py:19
  210.4 52.5 %all-to-all-start.3 = ((bf16[16,8,8192]{2,1,0:T(8,128)(2,1)}), bf16[16,8,8192]{2,1,0:T(8,128)(2,1)}, u32[]{:S(2)}, u32[]{:S(2)}) async-start(bf16[16,8,8192]{2,1,0:T(8,128)(2,1)} %fusion.5), calls=%async_computation.3 | async-start | bytes 4194304 | tf_op jit(solution)/shard_map/all_to_all | solution.py:77
  216.9 25.0 %copy-start.3 = (f32[64,8192]{1,0:T(8,128)}, f32[64,8192]{1,0:T(8,128)S(1)}, u32[]{:S(2)}) copy-start(f32[64,8192]{1,0:T(8,128)S(1)} %fusion.9) | copy-start | bytes 6291460
  217.0 25.0 %collective-permute-start.8 = (bf16[32,8192]{1,0:T(8,128)(2,1)S(1)}, bf16[32,8192]{1,0:T(8,128)(2,1)S(1)}, u32[]{:S(2)}, u32[]{:S(2)}) collective-permute-start(bf16[32,8192]{1,0:T(8,128)(2,1)S(1)} %dynamic-slice_convert_fusion), channel_id=1, source_target_pairs={{0,2},{1,3},{2,0},{3,1},{4,6},{5,7},{6,4},{7,5},{8,10},{9,11},{10,... | collective-permute-start | bytes 1572872 | tf_op jit(solution)/shard_map/ppermute | solution.py:19
  241.9 24.4 %copy-start.11 = (bf16[32,8192]{1,0:T(8,128)(2,1)}, bf16[32,8192]{1,0:T(8,128)(2,1)S(1)}, u32[]{:S(2)}) copy-start(bf16[32,8192]{1,0:T(8,128)(2,1)S(1)} %collective-permute-done.8) | copy-start | bytes 1572868
  242.1 22.7 %collective-permute-start.9 = (bf16[32,8192]{1,0:T(8,128)(2,1)S(1)}, bf16[32,8192]{1,0:T(8,128)(2,1)S(1)}, u32[]{:S(2)}, u32[]{:S(2)}) collective-permute-start(bf16[32,8192]{1,0:T(8,128)(2,1)S(1)} %fusion.19), channel_id=1, source_target_pairs={{0,4},{1,5},{2,6},{3,7},{12,8},{13,9},{14,10},{15,11},{16,20},{17,... | collective-permute-start | bytes 1572872 | tf_op jit(solution)/shard_map/ppermute | solution.py:50
  264.7 3.7 %copy-start.13 = (bf16[32,8192]{1,0:T(8,128)(2,1)}, bf16[32,8192]{1,0:T(8,128)(2,1)S(1)}, u32[]{:S(2)}) copy-start(bf16[32,8192]{1,0:T(8,128)(2,1)S(1)} %collective-permute-done.9) | copy-start | bytes 1572868
  266.4 15.2 %collective-permute-start.10 = (bf16[32,8192]{1,0:T(8,128)(2,1)S(1)}, bf16[32,8192]{1,0:T(8,128)(2,1)S(1)}, u32[]{:S(2)}, u32[]{:S(2)}) collective-permute-start(bf16[32,8192]{1,0:T(8,128)(2,1)S(1)} %fusion.15), channel_id=1, source_target_pairs={{4,8},{5,9},{6,10},{7,11},{8,4},{9,5},{10,6},{11,7},{20,24},{21,25... | collective-permute-start | bytes 1572872 | tf_op jit(solution)/shard_map/ppermute | solution.py:50
  272.8 8.8 %copy-start.4 = (f32[64,8192]{1,0:T(8,128)S(1)}, f32[64,8192]{1,0:T(8,128)}, u32[]{:S(2)}) copy-start(f32[64,8192]{1,0:T(8,128)} %copy-done.3) | copy-start | bytes 6291460
  272.8 8.8 %copy-start.12 = (bf16[32,8192]{1,0:T(8,128)(2,1)S(1)}, bf16[32,8192]{1,0:T(8,128)(2,1)}, u32[]{:S(2)}) copy-start(bf16[32,8192]{1,0:T(8,128)(2,1)} %copy-done.11) | copy-start | bytes 1572868
  272.8 8.8 %copy-start.14 = (bf16[32,8192]{1,0:T(8,128)(2,1)S(1)}, bf16[32,8192]{1,0:T(8,128)(2,1)}, u32[]{:S(2)}) copy-start(bf16[32,8192]{1,0:T(8,128)(2,1)} %copy-done.13) | copy-start | bytes 1572868
  282.7 13.1 %collective-permute-start.11 = (bf16[32,8192]{1,0:T(8,128)(2,1)}, bf16[32,8192]{1,0:T(8,128)(2,1)}, u32[]{:S(2)}, u32[]{:S(2)}) collective-permute-start(bf16[32,8192]{1,0:T(8,128)(2,1)} %add_convert_fusion), channel_id=1, source_target_pairs={{4,0},{5,1},{6,2},{7,3},{8,12},{9,13},{10,14},{11,15},{20,16},{21,... | collective-permute-start | bytes 1572872 | tf_op jit(solution)/shard_map/ppermute | solution.py:50
  288.2 5.7 %copy-start.15 = (bf16[128,8192]{1,0:T(8,128)(2,1)}, bf16[128,8192]{1,0:T(8,128)(2,1)S(1)}, u32[]{:S(2)}) copy-start(bf16[128,8192]{1,0:T(8,128)(2,1)S(1)} %fusion.1) | copy-start | bytes 6291460
  297.2 12.5 %collective-permute-start.12 = (bf16[32,8192]{1,0:T(8,128)(2,1)S(1)}, bf16[32,8192]{1,0:T(8,128)(2,1)S(1)}, u32[]{:S(2)}, u32[]{:S(2)}) collective-permute-start(bf16[32,8192]{1,0:T(8,128)(2,1)S(1)} %fusion.17), channel_id=1, source_target_pairs={{0,2},{1,3},{2,0},{3,1},{4,6},{5,7},{6,4},{7,5},{8,10},{9,11},{10,... | collective-permute-start | bytes 1572872 | tf_op jit(solution)/shard_map/ppermute | solution.py:19
  309.9 4.3 %collective-permute-start.13 = (bf16[64,8192]{1,0:T(8,128)(2,1)S(1)}, bf16[64,8192]{1,0:T(8,128)(2,1)S(1)}, u32[]{:S(2)}, u32[]{:S(2)}) collective-permute-start(bf16[64,8192]{1,0:T(8,128)(2,1)S(1)} %maximum_add_fusion.1), channel_id=1, source_target_pairs={{0,1},{1,0},{2,3},{3,2},{4,5},{5,4},{6,7},{7,6},{8,9},{9,8},{10,11... | collective-permute-start | bytes 3145736 | tf_op jit(solution)/shard_map/ppermute | solution.py:19
  314.3 2.0 copy-start.1
  (3 other events, 3.7 us)

commit v4 on v3

--- a/solution.py
+++ b/solution.py
@@ -64,11 +64,13 @@
 def sum_over_owner(x, me, owners, wire, ties):
     if owners & (owners - 1) or owners < 8:
         return lax.psum(x, "owner").astype(BF)
-    middle, third, last, final = ties
+    middle, third, final = ties
     x = halve(x, 0, me, owners, wire)
     x = halve(x, 1, me, owners, wire)
     x = line_sum(x, me, owners, 4, wire, middle).astype(BF)
-    x = double(after(after(x, third), last), 1, me, owners)
+    for other in third:
+        x = after(x, other)
+    x = double(x, 1, me, owners)
     return double(after(x, final), 0, me, owners)
 
 
@@ -116,11 +118,12 @@
     activated, hid_grad = gate(rows_by_rows(got_rows, down_mat), rows_by_rows(got_cot, up_mat))
     back_out = exchange(pick(activated, up_mat), owners)
     back_grad = exchange(pick(hid_grad, down_mat), owners)
-    own_sums = jnp.concatenate([outer_sum(hid_grad, got_rows), outer_sum(activated, got_cot)], 0).astype(BF)
+    own_down = outer_sum(hid_grad, got_rows).astype(BF)
+    own_up = outer_sum(activated, got_cot).astype(BF)
 
     both = jnp.concatenate([down_mat, up_mat], 0)
     both = jnp.where(me == busy, both, jnp.zeros_like(both))
-    both = sum_over_owner(both, me, owners, BF, (got_rows, got_cot, got_cot, back_out))
+    both = sum_over_owner(both, me, owners, BF, (got_rows, (got_cot,), back_out))
     busy_down, busy_up = both[:rank], both[rank:]
     busy_rows = pick(place_busy, tokens)
     busy_cot = pick(place_busy, cotangent)
@@ -133,9 +136,10 @@
 
     adapter_out = put(back_out, pick(busy_act, busy_up))
     input_grad = put(back_grad, pick(busy_hid, busy_down))
-    busy_sums = sum_over_owner(busy_sums, me, owners, BF, (back_grad, input_grad, adapter_out, own_sums))
-    sums = jnp.where(me == busy, busy_sums, own_sums)
-    return adapter_out, input_grad, sums[:rank][None], sums[rank:][None]
+    busy_sums = sum_over_owner(busy_sums, me, owners, BF, (back_grad, (input_grad, adapter_out, own_down, own_up), own_up))
+    down_sum = jnp.where(me == busy, busy_sums[:rank], own_down)
+    up_sum = jnp.where(me == busy, busy_sums[rank:], own_up)
+    return adapter_out, input_grad, down_sum[None], up_sum[None]
 
 
 def solution(mesh):

time: 320 us -> 320 us (level)
  waiting for transfers between devices: 200 us -> 196 us
    all_to_all x4, waiting for transfers between devices: 82.2 us -> 72.7 us  [exchange(): y = lax.all_to_all(y, 'owner', split_axis=0, concat_axis=0, tiled=True)]
    ppermute x8, waiting for transfers between devices: 59.8 us -> 65.1 us  [flip(): return lax.ppermute(x, 'owner', [(i, i ^ 1 << bit) for i in range(owners)])]
    slice x7 -> x8, local copies, waits for them, and re-layouts: 7 us -> 7.61 us  [after(): other[0, 0].astype(F32)]
where the time goes in v4:
time: 320 us; the launch traced here: 317 us
  waiting for transfers between devices  196 us (61%)
  starting transfers between devices  39.6 us (12%)
  matrix products  37.8 us (12%)
  other arithmetic  22.3 us (7%)
  local copies, waits for them, and re-layouts  13.6 us (4%)
  between operations  7.2 us (2%)
    all_to_all x4, waiting for transfers between devices, exchange(): y = lax.all_to_all(y, 'owner', split_axis=0, concat_axis=0, tiled=True)  72.7 us
    ppermute x8, waiting for transfers between devices, flip(): return lax.ppermute(x, 'owner', [(i, i ^ 1 << bit) for i in range(owners)])  65.1 us
    ppermute x6, waiting for transfers between devices, hop(): return lax.ppermute(y.astype(wire), 'owner', pairs).astype(x.dtype)  58.3 us
    all_to_all x4, starting transfers between devices, exchange(): y = lax.all_to_all(y, 'owner', split_axis=0, concat_axis=0, tiled=True)  22.7 us
    dot_general x8, matrix products, outer_sum(): lax.dot_general(a, b, (((0,), (0,)), ((), ())), preferred_element_type=F32)  21.5 us
    ppermute x6, starting transfers between devices, hop(): return lax.ppermute(y.astype(wire), 'owner', pairs).astype(x.dtype)  12.6 us
    dot_general x6, matrix products, pick(): return jnp.dot(which, rows, preferred_element_type=F32).astype(BF)  8.92 us
    slice x8, local copies, waits for them, and re-layouts, after(): other[0, 0].astype(F32)  7.61 us
  transfers between devices with their start and end apart: 18, of which 11 were waited for; matrix products, arithmetic and copies ran while one was open for 16% of the time, Pallas kernels for 0%

profile of v4, /device:TPU:11, one launch (start us, length us, event | category | flops | bytes accessed | tf_op | source)
XLA Modules:
  0.0 316.7 jit_solution(11948960551752967914)
XLA Ops:
  8.0 2.0 fusion.2
  10.0 6.4 %all-to-all-start = ((bf16[16,8,8192]{2,1,0:T(8,128)(2,1)}), bf16[16,8,8192]{2,1,0:T(8,128)(2,1)}, u32[]{:S(2)}, u32[]{:S(2)}) async-start(bf16[16,8,8192]{2,1,0:T(8,128)(2,1)} %fusion.2), calls=%async_computation | async-start | bytes 4194304 | tf_op jit(solution)/shard_map/all_to_all | solution.py:79
  19.3 2.0 fusion.3
  21.3 42.7 %all-to-all-done = bf16[16,8,8192]{2,1,0:T(8,128)(2,1)} async-done(((bf16[16,8,8192]{2,1,0:T(8,128)(2,1)}), bf16[16,8,8192]{2,1,0:T(8,128)(2,1)}, u32[]{:S(2)}, u32[]{:S(2)}) %all-to-all-start) | async-done | bytes 2097184 | tf_op jit(solution)/shard_map/all_to_all | solution.py:79
  64.0 4.9 %all-to-all-start.2 = ((bf16[16,8,8192]{2,1,0:T(8,128)(2,1)}), bf16[16,8,8192]{2,1,0:T(8,128)(2,1)}, u32[]{:S(2)}, u32[]{:S(2)}) async-start(bf16[16,8,8192]{2,1,0:T(8,128)(2,1)} %fusion.3), calls=%async_computation.2 | async-start | bytes 4194304 | tf_op jit(solution)/shard_map/all_to_all | solution.py:79
  73.3 42.5 %collective-permute-done.2 = bf16[32,8192]{1,0:T(8,128)(2,1)S(1)} collective-permute-done((bf16[32,8192]{1,0:T(8,128)(2,1)S(1)}, bf16[32,8192]{1,0:T(8,128)(2,1)S(1)}, u32[]{:S(2)}, u32[]{:S(2)}) %collective-permute-start.2) | collective-permute-done | bytes 524320 | tf_op jit(solution)/shard_map/ppermute | solution.py:50
  115.8 3.8 %collective-permute-start.3 = (bf16[32,8192]{1,0:T(8,128)(2,1)S(1)}, bf16[32,8192]{1,0:T(8,128)(2,1)S(1)}, u32[]{:S(2)}, u32[]{:S(2)}) collective-permute-start(bf16[32,8192]{1,0:T(8,128)(2,1)S(1)} %add_add_fusion.1), channel_id=1, source_target_pairs={{4,8},{5,9},{6,10},{7,11},{8,4},{9,5},{10,6},{11,7},{20,24},{21,25... | collective-permute-start | bytes 1572872 | tf_op jit(solution)/shard_map/ppermute | solution.py:50
  119.6 11.4 %collective-permute-done.3 = bf16[32,8192]{1,0:T(8,128)(2,1)S(1)} collective-permute-done((bf16[32,8192]{1,0:T(8,128)(2,1)S(1)}, bf16[32,8192]{1,0:T(8,128)(2,1)S(1)}, u32[]{:S(2)}, u32[]{:S(2)}) %collective-permute-start.3) | collective-permute-done | bytes 524320 | tf_op jit(solution)/shard_map/ppermute | solution.py:50
  131.9 2.1 collective-permute-start.4
  135.9 2.7 fusion.46
  138.6 2.1 fusion.4
  140.6 6.5 %all-to-all-start.1 = ((bf16[16,8,8192]{2,1,0:T(8,128)(2,1)}), bf16[16,8,8192]{2,1,0:T(8,128)(2,1)}, u32[]{:S(2)}, u32[]{:S(2)}) async-start(bf16[16,8,8192]{2,1,0:T(8,128)(2,1)} %fusion.4), calls=%async_computation.1 | async-start | bytes 4194304 | tf_op jit(solution)/shard_map/all_to_all | solution.py:79
  148.6 25.2 %collective-permute-done.5 = bf16[32,8192]{1,0:T(8,128)(2,1)S(1)} collective-permute-done((bf16[32,8192]{1,0:T(8,128)(2,1)S(1)}, bf16[32,8192]{1,0:T(8,128)(2,1)S(1)}, u32[]{:S(2)}, u32[]{:S(2)}) %collective-permute-start.5) | collective-permute-done | bytes 524320 | tf_op jit(solution)/shard_map/ppermute | solution.py:19
  174.8 19.9 %all-to-all-done.1 = bf16[16,8,8192]{2,1,0:T(8,128)(2,1)} async-done(((bf16[16,8,8192]{2,1,0:T(8,128)(2,1)}), bf16[16,8,8192]{2,1,0:T(8,128)(2,1)}, u32[]{:S(2)}, u32[]{:S(2)}) %all-to-all-start.1) | async-done | bytes 2097184 | tf_op jit(solution)/shard_map/all_to_all | solution.py:79
  205.9 2.4 fusion.11
  208.3 2.1 fusion.5
  210.4 4.9 %all-to-all-start.3 = ((bf16[16,8,8192]{2,1,0:T(8,128)(2,1)}), bf16[16,8,8192]{2,1,0:T(8,128)(2,1)}, u32[]{:S(2)}, u32[]{:S(2)}) async-start(bf16[16,8,8192]{2,1,0:T(8,128)(2,1)} %fusion.5), calls=%async_computation.3 | async-start | bytes 4194304 | tf_op jit(solution)/shard_map/all_to_all | solution.py:79
  217.3 24.6 %collective-permute-done.8 = bf16[32,8192]{1,0:T(8,128)(2,1)S(1)} collective-permute-done((bf16[32,8192]{1,0:T(8,128)(2,1)S(1)}, bf16[32,8192]{1,0:T(8,128)(2,1)S(1)}, u32[]{:S(2)}, u32[]{:S(2)}) %collective-permute-start.8) | collective-permute-done | bytes 524320 | tf_op jit(solution)/shard_map/ppermute | solution.py:19
  244.2 2.0 convolution_convert_fusion.4
  248.6 2.0 convolution_convert_fusion.5
  252.8 10.1 %all-to-all-done.3 = bf16[16,8,8192]{2,1,0:T(8,128)(2,1)} async-done(((bf16[16,8,8192]{2,1,0:T(8,128)(2,1)}), bf16[16,8,8192]{2,1,0:T(8,128)(2,1)}, u32[]{:S(2)}, u32[]{:S(2)}) %all-to-all-start.3) | async-done | bytes 2097184 | tf_op jit(solution)/shard_map/all_to_all | solution.py:79
  266.1 2.1 collective-permute-start.10
  268.2 4.4 %fusion.25 = f32[128,8192]{1,0:T(8,128)} fusion(pred[152,128]{1,0:T(8,128)(4,1)S(1)} %iota_compare_fusion, bf16[16,8,8192]{2,1,0:T(8,128)(2,1)} %all-to-all-done.3), kind=kOutput, calls=%fused_computation.67 | convolution fusion | flops 268435456 | bytes 6307840 | tf_op jit(solution)/shard_map/dot_general | solution.py:15
  272.6 4.3 %fusion.28 = f32[128,8192]{1,0:T(8,128)} fusion(pred[152,128]{1,0:T(8,128)(4,1)S(1)} %iota_compare_fusion, bf16[16,8,8192]{2,1,0:T(8,128)(2,1)} %all-to-all-done.1), kind=kOutput, calls=%fused_computation.70 | convolution fusion | flops 268435456 | bytes 6307840 | tf_op jit(solution)/shard_map/dot_general | solution.py:15
  276.9 4.4 %collective-permute-done.10 = bf16[32,8192]{1,0:T(8,128)(2,1)S(1)} collective-permute-done((bf16[32,8192]{1,0:T(8,128)(2,1)S(1)}, bf16[32,8192]{1,0:T(8,128)(2,1)S(1)}, u32[]{:S(2)}, u32[]{:S(2)}) %collective-permute-start.10) | collective-permute-done | bytes 524320 | tf_op jit(solution)/shard_map/ppermute | solution.py:50
  281.4 2.2 add_convert_fusion
  283.5 2.1 collective-permute-start.11
  285.6 3.4 %fusion.1 = bf16[128,8192]{1,0:T(8,128)(2,1)S(1)} fusion(f32[128,8192]{1,0:T(8,128)} %fusion.25, bf16[24,64]{1,0:T(8,128)(2,1)S(1)} %fusion.13, bf16[64,8192]{1,0:T(8,128)(2,1)S(1)} %maximum_add_fusion, bf16[64,8192]{1,0:T(8,128)(2,1)} %collective-permute-done.6, pred[]{:T(512)S(6)} %eq.71, pred[152,128]{1,0:T(8,128)(4,1)S(1)} %iota_compare_fusion), kind=kOutput, calls=%fused_computation.3 | convolution fusion | flops 78315520 | bytes 8397825 | tf_op jit(solution)/shard_map/dot_general | solution.py:15
  290.3 4.4 %fusion = bf16[128,8192]{1,0:T(8,128)(2,1)} fusion(f32[128,8192]{1,0:T(8,128)} %fusion.28, bf16[64,8192]{1,0:T(8,128)(2,1)} %collective-permute-done.6, bf16[64,8192]{1,0:T(8,128)(2,1)S(1)} %maximum_add_fusion, pred[]{:T(512)S(6)} %eq.71, pred[152,128]{1,0:T(8,128)(4,1)S(1)} %iota_compare_fusion, f32[24,64]{1,0:T(8,128)S(1)} %fusion.20), kind=kOutput, calls=%fused_computation.2 | convolution fusion | flops 78323200 | bytes 8403969 | tf_op jit(solution)/shard_map/dot_general | solution.py:15
  298.2 12.4 %collective-permute-done.12 = bf16[32,8192]{1,0:T(8,128)(2,1)S(1)} collective-permute-done((bf16[32,8192]{1,0:T(8,128)(2,1)S(1)}, bf16[32,8192]{1,0:T(8,128)(2,1)S(1)}, u32[]{:S(2)}, u32[]{:S(2)}) %collective-permute-start.12) | collective-permute-done | bytes 524320 | tf_op jit(solution)/shard_map/ppermute | solution.py:19
  310.9 2.0 collective-permute-start.13
  312.9 2.3 collective-permute-done.13
  (94 shorter events, 43.2 us)
Async XLA Ops:
  0.6 18.7 %copy-start = (bf16[128,8192]{1,0:T(8,128)(2,1)S(1)}, bf16[128,8192]{1,0:T(8,128)(2,1)}, u32[]{:S(2)}) copy-start(bf16[128,8192]{1,0:T(8,128)(2,1)} %param.7) | copy-start | bytes 6291460
  6.2 1.7 copy-start.8
  6.3 10.1 %collective-permute-start = (bf16[64,8192]{1,0:T(8,128)(2,1)S(1)}, bf16[64,8192]{1,0:T(8,128)(2,1)}, u32[]{:S(2)}, u32[]{:S(2)}) collective-permute-start(bf16[64,8192]{1,0:T(8,128)(2,1)S(1)} %constant_dynamic-slice_fusion.1), channel_id=1, source_target_pairs={{0,1},{1,0},{2,3},{3,2},{4,5},{5,4},{6,7},{7,6},{8,9},{9,8},{10,11... | collective-permute-start | bytes 3145736 | tf_op jit(solution)/shard_map/ppermute | solution.py:19
  10.0 54.0 %all-to-all-start = ((bf16[16,8,8192]{2,1,0:T(8,128)(2,1)}), bf16[16,8,8192]{2,1,0:T(8,128)(2,1)}, u32[]{:S(2)}, u32[]{:S(2)}) async-start(bf16[16,8,8192]{2,1,0:T(8,128)(2,1)} %fusion.2), calls=%async_computation | async-start | bytes 4194304 | tf_op jit(solution)/shard_map/all_to_all | solution.py:79
  19.0 49.9 %collective-permute-start.1 = (bf16[32,8192]{1,0:T(8,128)(2,1)}, bf16[32,8192]{1,0:T(8,128)(2,1)}, u32[]{:S(2)}, u32[]{:S(2)}) collective-permute-start(bf16[32,8192]{1,0:T(8,128)(2,1)} %constant_dynamic-slice_fusion), channel_id=1, source_target_pairs={{0,2},{1,3},{2,0},{3,1},{4,6},{5,7},{6,4},{7,5},{8,10},{9,11},{10,... | collective-permute-start | bytes 1572872 | tf_op jit(solution)/shard_map/ppermute | solution.py:19
  64.0 70.0 %all-to-all-start.2 = ((bf16[16,8,8192]{2,1,0:T(8,128)(2,1)}), bf16[16,8,8192]{2,1,0:T(8,128)(2,1)}, u32[]{:S(2)}, u32[]{:S(2)}) async-start(bf16[16,8,8192]{2,1,0:T(8,128)(2,1)} %fusion.3), calls=%async_computation.2 | async-start | bytes 4194304 | tf_op jit(solution)/shard_map/all_to_all | solution.py:79
  70.1 45.6 %collective-permute-start.2 = (bf16[32,8192]{1,0:T(8,128)(2,1)S(1)}, bf16[32,8192]{1,0:T(8,128)(2,1)S(1)}, u32[]{:S(2)}, u32[]{:S(2)}) collective-permute-start(bf16[32,8192]{1,0:T(8,128)(2,1)S(1)} %dynamic-slice_add_fusion.1), channel_id=1, source_target_pairs={{0,4},{1,5},{2,6},{3,7},{12,8},{13,9},{14,10},{15,11},{16,20},{17,... | collective-permute-start | bytes 1572872 | tf_op jit(solution)/shard_map/ppermute | solution.py:50
  115.8 22.8 %copy-start.5 = (bf16[1,64,8192]{2,1,0:T(8,128)(2,1)S(1)}, bf16[1,64,8192]{2,1,0:T(8,128)(2,1)}, u32[]{:S(2)}) copy-start(bf16[1,64,8192]{2,1,0:T(8,128)(2,1)} %param.9) | copy-start | bytes 3145732
  115.8 15.2 %collective-permute-start.3 = (bf16[32,8192]{1,0:T(8,128)(2,1)S(1)}, bf16[32,8192]{1,0:T(8,128)(2,1)S(1)}, u32[]{:S(2)}, u32[]{:S(2)}) collective-permute-start(bf16[32,8192]{1,0:T(8,128)(2,1)S(1)} %add_add_fusion.1), channel_id=1, source_target_pairs={{4,8},{5,9},{6,10},{7,11},{8,4},{9,5},{10,6},{11,7},{20,24},{21,25... | collective-permute-start | bytes 1572872 | tf_op jit(solution)/shard_map/ppermute | solution.py:50
  131.9 15.2 %collective-permute-start.4 = (bf16[32,8192]{1,0:T(8,128)(2,1)}, bf16[32,8192]{1,0:T(8,128)(2,1)}, u32[]{:S(2)}, u32[]{:S(2)}) collective-permute-start(bf16[32,8192]{1,0:T(8,128)(2,1)} %add.154), channel_id=1, source_target_pairs={{4,0},{5,1},{6,2},{7,3},{8,12},{9,13},{10,14},{11,15},{20,16},{21,... | collective-permute-start | bytes 1572872 | tf_op jit(solution)/shard_map/ppermute | solution.py:50
  140.6 54.1 %all-to-all-start.1 = ((bf16[16,8,8192]{2,1,0:T(8,128)(2,1)}), bf16[16,8,8192]{2,1,0:T(8,128)(2,1)}, u32[]{:S(2)}, u32[]{:S(2)}) async-start(bf16[16,8,8192]{2,1,0:T(8,128)(2,1)} %fusion.4), calls=%async_computation.1 | async-start | bytes 4194304 | tf_op jit(solution)/shard_map/all_to_all | solution.py:79
  148.2 25.5 %collective-permute-start.5 = (bf16[32,8192]{1,0:T(8,128)(2,1)S(1)}, bf16[32,8192]{1,0:T(8,128)(2,1)S(1)}, u32[]{:S(2)}, u32[]{:S(2)}) collective-permute-start(bf16[32,8192]{1,0:T(8,128)(2,1)S(1)} %select_add_fusion), channel_id=1, source_target_pairs={{0,2},{1,3},{2,0},{3,1},{4,6},{5,7},{6,4},{7,5},{8,10},{9,11},{10,... | collective-permute-start | bytes 1572872 | tf_op jit(solution)/shard_map/ppermute | solution.py:19
  198.0 2.9 collective-permute-start.6
  203.8 1.7 copy-start.2
  203.9 2.0 copy-start.6
  205.5 2.8 copy-start.7
  205.5 9.8 %collective-permute-start.7 = (bf16[64,8192]{1,0:T(8,128)(2,1)}, bf16[64,8192]{1,0:T(8,128)(2,1)}, u32[]{:S(2)}, u32[]{:S(2)}) collective-permute-start(bf16[64,8192]{1,0:T(8,128)(2,1)} %fusion.7), channel_id=1, source_target_pairs={{0,1},{1,0},{2,3},{3,2},{4,5},{5,4},{6,7},{7,6},{8,9},{9,8},{10,11... | collective-permute-start | bytes 3145736 | tf_op jit(solution)/shard_map/ppermute | solution.py:19
  210.4 52.5 %all-to-all-start.3 = ((bf16[16,8,8192]{2,1,0:T(8,128)(2,1)}), bf16[16,8,8192]{2,1,0:T(8,128)(2,1)}, u32[]{:S(2)}, u32[]{:S(2)}) async-start(bf16[16,8,8192]{2,1,0:T(8,128)(2,1)} %fusion.5), calls=%async_computation.3 | async-start | bytes 4194304 | tf_op jit(solution)/shard_map/all_to_all | solution.py:79
  216.9 29.4 %copy-start.3 = (f32[64,8192]{1,0:T(8,128)}, f32[64,8192]{1,0:T(8,128)S(1)}, u32[]{:S(2)}) copy-start(f32[64,8192]{1,0:T(8,128)S(1)} %fusion.9) | copy-start | bytes 6291460
  217.0 25.0 %collective-permute-start.8 = (bf16[32,8192]{1,0:T(8,128)(2,1)S(1)}, bf16[32,8192]{1,0:T(8,128)(2,1)S(1)}, u32[]{:S(2)}, u32[]{:S(2)}) collective-permute-start(bf16[32,8192]{1,0:T(8,128)(2,1)S(1)} %dynamic-slice_convert_fusion), channel_id=1, source_target_pairs={{0,2},{1,3},{2,0},{3,1},{4,6},{5,7},{6,4},{7,5},{8,10},{9,11},{10,... | collective-permute-start | bytes 1572872 | tf_op jit(solution)/shard_map/ppermute | solution.py:19
  241.9 4.4 %copy-start.11 = (bf16[32,8192]{1,0:T(8,128)(2,1)}, bf16[32,8192]{1,0:T(8,128)(2,1)S(1)}, u32[]{:S(2)}) copy-start(bf16[32,8192]{1,0:T(8,128)(2,1)S(1)} %collective-permute-done.8) | copy-start | bytes 1572868
  242.9 21.8 %collective-permute-start.9 = (bf16[32,8192]{1,0:T(8,128)(2,1)}, bf16[32,8192]{1,0:T(8,128)(2,1)}, u32[]{:S(2)}, u32[]{:S(2)}) collective-permute-start(bf16[32,8192]{1,0:T(8,128)(2,1)} %fusion.21), channel_id=1, source_target_pairs={{0,4},{1,5},{2,6},{3,7},{12,8},{13,9},{14,10},{15,11},{16,20},{17,... | collective-permute-start | bytes 1572872 | tf_op jit(solution)/shard_map/ppermute | solution.py:50
  247.8 17.0 %copy-start.4 = (f32[64,8192]{1,0:T(8,128)S(1)}, f32[64,8192]{1,0:T(8,128)}, u32[]{:S(2)}) copy-start(f32[64,8192]{1,0:T(8,128)} %copy-done.3) | copy-start | bytes 6291460
  266.1 15.2 %collective-permute-start.10 = (bf16[32,8192]{1,0:T(8,128)(2,1)S(1)}, bf16[32,8192]{1,0:T(8,128)(2,1)S(1)}, u32[]{:S(2)}, u32[]{:S(2)}) collective-permute-start(bf16[32,8192]{1,0:T(8,128)(2,1)S(1)} %fusion.15), channel_id=1, source_target_pairs={{4,8},{5,9},{6,10},{7,11},{8,4},{9,5},{10,6},{11,7},{20,24},{21,25... | collective-permute-start | bytes 1572872 | tf_op jit(solution)/shard_map/ppermute | solution.py:50
  272.6 8.8 %copy-start.12 = (bf16[32,8192]{1,0:T(8,128)(2,1)S(1)}, bf16[32,8192]{1,0:T(8,128)(2,1)}, u32[]{:S(2)}) copy-start(bf16[32,8192]{1,0:T(8,128)(2,1)} %copy-done.11) | copy-start | bytes 1572868
  283.5 13.1 %collective-permute-start.11 = (bf16[32,8192]{1,0:T(8,128)(2,1)}, bf16[32,8192]{1,0:T(8,128)(2,1)}, u32[]{:S(2)}, u32[]{:S(2)}) collective-permute-start(bf16[32,8192]{1,0:T(8,128)(2,1)} %add_convert_fusion), channel_id=1, source_target_pairs={{4,0},{5,1},{6,2},{7,3},{8,12},{9,13},{10,14},{11,15},{20,16},{21,... | collective-permute-start | bytes 1572872 | tf_op jit(solution)/shard_map/ppermute | solution.py:50
  289.0 5.7 %copy-start.17 = (bf16[128,8192]{1,0:T(8,128)(2,1)}, bf16[128,8192]{1,0:T(8,128)(2,1)S(1)}, u32[]{:S(2)}) copy-start(bf16[128,8192]{1,0:T(8,128)(2,1)S(1)} %fusion.1) | copy-start | bytes 6291460
  298.1 17.1 %copy-start.14 = (bf16[64,8192]{1,0:T(8,128)(2,1)S(1)}, bf16[64,8192]{1,0:T(8,128)(2,1)}, u32[]{:S(2)}) copy-start(bf16[64,8192]{1,0:T(8,128)(2,1)} %copy-done.13) | copy-start | bytes 3145732
  298.1 17.0 %copy-start.16 = (bf16[64,8192]{1,0:T(8,128)(2,1)S(1)}, bf16[64,8192]{1,0:T(8,128)(2,1)}, u32[]{:S(2)}) copy-start(bf16[64,8192]{1,0:T(8,128)(2,1)} %copy-done.15) | copy-start | bytes 3145732
  298.1 12.5 %collective-permute-start.12 = (bf16[32,8192]{1,0:T(8,128)(2,1)S(1)}, bf16[32,8192]{1,0:T(8,128)(2,1)S(1)}, u32[]{:S(2)}, u32[]{:S(2)}) collective-permute-start(bf16[32,8192]{1,0:T(8,128)(2,1)S(1)} %fusion.19), channel_id=1, source_target_pairs={{0,2},{1,3},{2,0},{3,1},{4,6},{5,7},{6,4},{7,5},{8,10},{9,11},{10,... | collective-permute-start | bytes 1572872 | tf_op jit(solution)/shard_map/ppermute | solution.py:19
  310.7 6.0 %copy-start.1 = (bf16[128,8192]{1,0:T(8,128)(2,1)S(1)}, bf16[128,8192]{1,0:T(8,128)(2,1)}, u32[]{:S(2)}) copy-start(bf16[128,8192]{1,0:T(8,128)(2,1)} %param.7) | copy-start | bytes 6291460
  310.9 4.3 %collective-permute-start.13 = (bf16[64,8192]{1,0:T(8,128)(2,1)S(1)}, bf16[64,8192]{1,0:T(8,128)(2,1)S(1)}, u32[]{:S(2)}, u32[]{:S(2)}) collective-permute-start(bf16[64,8192]{1,0:T(8,128)(2,1)S(1)} %maximum_add_fusion.1), channel_id=1, source_target_pairs={{0,1},{1,0},{2,3},{3,2},{4,5},{5,4},{6,7},{7,6},{8,9},{9,8},{10,11... | collective-permute-start | bytes 3145736 | tf_op jit(solution)/shard_map/ppermute | solution.py:19
  (5 other events, 5.7 us)
